TPU v7x, 512 devices: a whole 4x8x8 slice. The times are simulated.
512 devices in a mesh: dir: 8 (over z), gx: 64 (over x, y, core).
Axes of the slice: x: 4, y: 8, z: 8, core: 2. Of those that a mesh axis runs over, the one named last changes fastest.
Arguments:
- cotangent: float32 [8, 256, 32, 512], P('dir', 'gx'), may hold values from -24 to 24
- potential: float32 [8, 256, 32, 512], P('dir', 'gx'), may hold values from -0.6 to 0.6
- height: float32 [256, 512], P('gx'), may hold values from 0 to 1
Outputs:
- adjoint: float32 [8, 256, 32, 512], P('dir', 'gx')
- gradient: float32 [256, 512], P('gx', 'dir')
All inputs are finite; a program needn't handle non-finite values.
Results may differ from a plain program's by a relative error of at most 0.0002.
Values sent between devices are 32-bit elements; how exact they have to be, the bound alone decides.
A program may use at most 64 MiB of HBM per device.

v0:
```python
import jax
import jax.numpy as jnp
from jax import lax
from jax.sharding import PartitionSpec as P

LEVELS = 3
SWEEPS = 2
COARSE_SWEEPS = 8


damping = 0.7
anisotropy = 4.0
ceiling = 1.5


def padded(block, sides, width):
    for axis, dim in sides:
        count = lax.axis_size(axis)
        forward = [(i, i + 1) for i in range(count - 1)]
        backward = [(target, source) for source, target in forward]
        low = lax.ppermute(
            lax.slice_in_dim(block, block.shape[dim] - width, None, axis=dim), axis, forward
        )
        high = lax.ppermute(lax.slice_in_dim(block, 0, width, axis=dim), axis, backward)
        block = jnp.concatenate([low, block, high], axis=dim)
    return block


def safe_harmonic(first_side, second_side, factor):
    summed = first_side + second_side
    safe_sum = jnp.where(summed > 0, summed, 1.0)
    return factor * 2.0 * first_side * second_side / safe_sum


def side_sum(weights, axis_pos):
    pad_before = [(0, 0)] * weights.ndim
    pad_after = [(0, 0)] * weights.ndim
    pad_before[axis_pos] = (1, 0)
    pad_after[axis_pos] = (0, 1)
    return jnp.pad(weights, pad_before) + jnp.pad(weights, pad_after)


def level_data(terrain, factor, rim_width):
    x_faces = safe_harmonic(terrain[:-1], terrain[1:], factor)
    y_faces = safe_harmonic(terrain[:, :-1], terrain[:, 1:], factor)
    positive = terrain > 0
    z_weight = jnp.where(positive, factor * anisotropy / jnp.where(positive, terrain, 1.0), 0.0)
    centre = side_sum(x_faces, 0) + side_sum(y_faces, 1)
    return (x_faces, y_faces, z_weight, centre, rim_width)


def diagonal_rows(operator, first_row, row_count, depth_count):
    x_faces, y_faces, z_weight, centre, rim_width = operator
    layer_weight = jnp.where(jnp.arange(depth_count) == 0, 1.0, 2.0)
    centre_rows = centre[first_row : first_row + row_count][:, None, :]
    z_rows = z_weight[first_row : first_row + row_count][:, None, :]
    return centre_rows + z_rows * layer_weight[None, :, None]


def apply_rows(estimate, margin, operator):
    x_faces, y_faces, z_weight, centre, rim_width = operator
    row_count = estimate.shape[0] - 2
    first_row = rim_width - margin + 1
    middle = estimate[1:-1]
    diagonal = diagonal_rows(operator, first_row, row_count, estimate.shape[1])
    west_weight = x_faces[first_row - 1 : first_row - 1 + row_count][:, None, :]
    east_weight = x_faces[first_row : first_row + row_count][:, None, :]
    y_weight = y_faces[first_row : first_row + row_count][:, None, :]
    z_rows = z_weight[first_row : first_row + row_count][:, None, :]
    y_terms = jnp.pad(y_weight * middle[:, :, 1:], ((0, 0), (0, 0), (0, 1))) + jnp.pad(
        y_weight * middle[:, :, :-1], ((0, 0), (0, 0), (1, 0))
    )
    z_terms = z_rows * (
        jnp.pad(middle[:, 1:], ((0, 0), (0, 1), (0, 0)))
        + jnp.pad(middle[:, :-1], ((0, 0), (1, 0), (0, 0)))
    )
    applied = (
        diagonal * middle
        - west_weight * estimate[:-2]
        - east_weight * estimate[2:]
        - y_terms
        - z_terms
    )
    return (applied, diagonal)


def jacobi(estimate, margin, forcing, operator):
    applied, diagonal = apply_rows(estimate, margin, operator)
    diagonal = jnp.where(diagonal > 0, diagonal, 1.0)
    return estimate[1:-1] + damping * (forcing - applied) / diagonal


def restrict(fine_values):
    extent = fine_values.shape
    return fine_values.reshape(extent[0] // 2, 2, extent[1] // 2, 2, extent[2] // 2, 2).sum(
        axis=(1, 3, 5)
    )


def prolong(coarse_values):
    return jnp.repeat(jnp.repeat(jnp.repeat(coarse_values, 2, 0), 2, 1), 2, 2)


def shrink(terrain):
    extent = terrain.shape
    return terrain.reshape(extent[0] // 2, 2, extent[1] // 2, 2).mean(axis=(1, 3))


def coarsest(forcing, estimate, operator):
    for sweep_index in range(COARSE_SWEEPS - 1):
        estimate = jacobi(padded(estimate, (("gx", 0),), 1), 1, forcing, operator)
    return estimate


def vcycle(forcing, depth_level, terrain, rim_width):
    operator = level_data(terrain, 2.0**depth_level, rim_width)
    strip_rows = forcing.shape[0]
    estimate = damping * forcing / diagonal_rows(operator, rim_width, strip_rows, forcing.shape[1])
    if depth_level == LEVELS - 1:
        return coarsest(forcing, estimate, operator)
    estimate = jacobi(padded(estimate, (("gx", 0),), 1), 1, forcing, operator)
    applied, unused = apply_rows(padded(estimate, (("gx", 0),), 1), 1, operator)
    correction = vcycle(
        restrict(forcing - applied), depth_level + 1, shrink(terrain), rim_width // 2
    )
    estimate = estimate + prolong(correction)
    for sweep_index in range(SWEEPS):
        estimate = jacobi(padded(estimate, (("gx", 0),), 1), 1, forcing, operator)
    return estimate


def terrain_term(adjoint, potential, depth_map, rim_width):
    strip_rows = adjoint.shape[0]
    own_depth = depth_map[rim_width : rim_width + strip_rows]
    stacked = padded(jnp.stack((adjoint, potential)), (("gx", 1),), 1)
    wide_adjoint = stacked[0]
    wide_potential = stacked[1]
    x_prod = jnp.sum(
        (wide_adjoint[1:] - wide_adjoint[:-1]) * (wide_potential[1:] - wide_potential[:-1]), axis=1
    )
    west_depth = depth_map[rim_width - 1 : rim_width + strip_rows]
    east_depth = depth_map[rim_width : rim_width + strip_rows + 1]
    summed = (west_depth + east_depth) * (west_depth + east_depth)
    west_share = 2.0 * east_depth * east_depth / summed * x_prod
    east_share = 2.0 * west_depth * west_depth / summed * x_prod
    x_term = west_share[1:] + east_share[:-1]
    y_prod = jnp.sum(
        (adjoint[:, :, 1:] - adjoint[:, :, :-1]) * (potential[:, :, 1:] - potential[:, :, :-1]),
        axis=1,
    )
    south_depth = own_depth[:, :-1]
    north_depth = own_depth[:, 1:]
    y_summed = (south_depth + north_depth) * (south_depth + north_depth)
    south_share = 2.0 * north_depth * north_depth / y_summed * y_prod
    north_share = 2.0 * south_depth * south_depth / y_summed * y_prod
    y_term = jnp.pad(south_share, ((0, 0), (0, 1))) + jnp.pad(north_share, ((0, 0), (1, 0)))
    z_prod = (
        jnp.sum((adjoint[:, 1:] - adjoint[:, :-1]) * (potential[:, 1:] - potential[:, :-1]), axis=1)
        + adjoint[:, -1] * potential[:, -1]
    )
    z_term = -anisotropy / (own_depth * own_depth) * z_prod
    return x_term + y_term + z_term


def body(cotangent, potential, height):
    rim_width = 2 ** (LEVELS - 1)
    depth_map = padded(ceiling - height, (("gx", 0),), rim_width)
    adjoint = vcycle(cotangent[0], 0, depth_map, rim_width)
    dir_term = terrain_term(adjoint, potential[0], depth_map, rim_width)
    gradient = lax.psum_scatter(dir_term, "dir", scatter_dimension=1, tiled=True)
    return (adjoint[None], gradient)


def solution(mesh):
    placed = (P("dir", "gx", None, None), P("dir", "gx", None, None), P("gx", None))
    return jax.shard_map(
        body,
        mesh=mesh,
        in_specs=placed,
        out_specs=(P("dir", "gx", None, None), P("gx", "dir")),
        check_vma=False,
    )
```

profile of v0, /device:TPU:6, one launch (start us, length us, event | category | flops | bytes accessed | tf_op | source)
XLA Modules:
  0.0 279.4 jit_solution(2973538090125263642)
XLA Ops:
  9.8 5.8 %collective-permute-start.1 = (f32[4,512]{1,0:T(4,128)S(1)}, f32[4,512]{1,0:T(4,128)S(1)}, u32[]{:S(2)}, u32[]{:S(2)}) collective-permute-start(f32[4,512]{1,0:T(4,128)S(1)} %broadcast_subtract_fusion), channel_id=1, source_target_pairs={{1,0},{2,1},{3,2},{4,3},{5,4},{6,5},{7,6},{8,7},{9,8},{10,9},{11,1... | collective-permute-start | bytes 24584 | tf_op jit(solution)/shard_map/ppermute | solution.py:24
  16.9 2.3 copy.57
  21.8 2.7 reshape.386
  29.3 5.8 %collective-permute-start.3 = (f32[1,32,512]{1,2,0:T(8,128)S(1)}, f32[1,32,512]{1,2,0:T(8,128)S(1)}, u32[]{:S(2)}, u32[]{:S(2)}) collective-permute-start(f32[1,32,512]{1,2,0:T(8,128)S(1)} %get-tuple-element.25), channel_id=1, source_target_pairs={{1,0},{2,1},{3,2},{4,3},{5,4},{6,5},{7,6},{8,7},{9,8},{10,9},{11,1... | collective-permute-start | bytes 196616 | tf_op jit(solution)/shard_map/ppermute | solution.py:24
  38.9 3.4 %fusion.39 = f32[4,32,512]{1,2,0:T(8,128)S(1)} fusion(f32[4,32,512]{1,2,0:T(8,128)S(1)} %fusion.42, f32[1,32,512]{1,2,0:T(8,128)S(1)} %collective-permute-done.3, f32[1,32,512]{1,2,0:T(8,128)S(1)} %collective-permute-done.2, f32[1,4,32,512]{2,3,1,0:T(8,128)S(1)} %copy.50, f32[4,31,512]{1,2,0:T(8,128)} %get-tuple-element.23, ...), kind=kLoop, calls=%fused_computation.60 | loop fusion | flops 1310720 | bytes 1981568 | tf_op jit(solution)/shard_map/add | solution.py:90
  44.7 5.9 %collective-permute-start.5 = (f32[1,32,512]{1,2,0:T(8,128)S(1)}, f32[1,32,512]{1,2,0:T(8,128)S(1)}, u32[]{:S(2)}, u32[]{:S(2)}) collective-permute-start(f32[1,32,512]{1,2,0:T(8,128)S(1)} %get-tuple-element.21), channel_id=1, source_target_pairs={{1,0},{2,1},{3,2},{4,3},{5,4},{6,5},{7,6},{8,7},{9,8},{10,9},{11,1... | collective-permute-start | bytes 196616 | tf_op jit(solution)/shard_map/ppermute | solution.py:24
  56.5 18.1 %reshape.385 = f32[2,2,16,2,256,2]{5,4,3,2,1,0:T(8,128)} reshape(f32[4,32,512]{2,1,0:T(8,128)S(1)} %copy.51) | data formatting | bytes 524288 | tf_op jit(solution)/shard_map/reshape | solution.py:95
  74.6 7.0 %reduce_sum.72 = f32[2,16,256]{2,1,0:T(8,128)S(1)} reduce(f32[2,2,16,2,256,2]{5,4,3,2,1,0:T(8,128)} %reshape.385, f32[]{:T(128)} %constant.14.clone.1), dimensions={1,3,5}, to_apply=%region_0.1 | reduce | flops 57344 | bytes 294916 | tf_op jit(solution)/shard_map/reduce_sum | solution.py:95
  83.7 5.9 %collective-permute-start.7 = (f32[1,16,256]{2,1,0:T(8,128)S(1)}, f32[1,16,256]{2,1,0:T(8,128)S(1)}, u32[]{:S(2)}, u32[]{:S(2)}) collective-permute-start(f32[1,16,256]{2,1,0:T(8,128)S(1)} %get-tuple-element.53), channel_id=1, source_target_pairs={{1,0},{2,1},{3,2},{4,3},{5,4},{6,5},{7,6},{8,7},{9,8},{10,9},{11,1... | collective-permute-start | bytes 49160 | tf_op jit(solution)/shard_map/ppermute | solution.py:24
  93.1 5.8 %collective-permute-start.9 = (f32[1,16,256]{2,1,0:T(8,128)S(1)}, f32[1,16,256]{2,1,0:T(8,128)S(1)}, u32[]{:S(2)}, u32[]{:S(2)}) collective-permute-start(f32[1,16,256]{2,1,0:T(8,128)S(1)} %get-tuple-element.49), channel_id=1, source_target_pairs={{1,0},{2,1},{3,2},{4,3},{5,4},{6,5},{7,6},{8,7},{9,8},{10,9},{11,1... | collective-permute-start | bytes 49160 | tf_op jit(solution)/shard_map/ppermute | solution.py:24
  103.6 5.8 %collective-permute-start.11 = (f32[1,8,128]{2,1,0:T(8,128)S(1)}, f32[1,8,128]{2,1,0:T(8,128)S(1)}, u32[]{:S(2)}, u32[]{:S(2)}) collective-permute-start(f32[1,8,128]{2,1,0:T(8,128)S(1)} %fusion.102), channel_id=1, source_target_pairs={{1,0},{2,1},{3,2},{4,3},{5,4},{6,5},{7,6},{8,7},{9,8},{10,9},{11,1... | collective-permute-start | bytes 12296 | tf_op jit(solution)/shard_map/ppermute | solution.py:24
  112.8 5.8 %collective-permute-start.13 = (f32[1,8,128]{2,1,0:T(8,128)S(1)}, f32[1,8,128]{2,1,0:T(8,128)S(1)}, u32[]{:S(2)}, u32[]{:S(2)}) collective-permute-start(f32[1,8,128]{2,1,0:T(8,128)S(1)} %fusion.105), channel_id=1, source_target_pairs={{1,0},{2,1},{3,2},{4,3},{5,4},{6,5},{7,6},{8,7},{9,8},{10,9},{11,1... | collective-permute-start | bytes 12296 | tf_op jit(solution)/shard_map/ppermute | solution.py:24
  121.9 5.8 %collective-permute-start.15 = (f32[1,8,128]{2,1,0:T(8,128)S(1)}, f32[1,8,128]{2,1,0:T(8,128)S(1)}, u32[]{:S(2)}, u32[]{:S(2)}) collective-permute-start(f32[1,8,128]{2,1,0:T(8,128)S(1)} %fusion.108), channel_id=1, source_target_pairs={{1,0},{2,1},{3,2},{4,3},{5,4},{6,5},{7,6},{8,7},{9,8},{10,9},{11,1... | collective-permute-start | bytes 12296 | tf_op jit(solution)/shard_map/ppermute | solution.py:24
  131.1 5.8 %collective-permute-start.17 = (f32[1,8,128]{2,1,0:T(8,128)S(1)}, f32[1,8,128]{2,1,0:T(8,128)S(1)}, u32[]{:S(2)}, u32[]{:S(2)}) collective-permute-start(f32[1,8,128]{2,1,0:T(8,128)S(1)} %fusion.111), channel_id=1, source_target_pairs={{1,0},{2,1},{3,2},{4,3},{5,4},{6,5},{7,6},{8,7},{9,8},{10,9},{11,1... | collective-permute-start | bytes 12296 | tf_op jit(solution)/shard_map/ppermute | solution.py:24
  140.2 5.8 %collective-permute-start.19 = (f32[1,8,128]{2,1,0:T(8,128)S(1)}, f32[1,8,128]{2,1,0:T(8,128)S(1)}, u32[]{:S(2)}, u32[]{:S(2)}) collective-permute-start(f32[1,8,128]{2,1,0:T(8,128)S(1)} %fusion.114), channel_id=1, source_target_pairs={{1,0},{2,1},{3,2},{4,3},{5,4},{6,5},{7,6},{8,7},{9,8},{10,9},{11,1... | collective-permute-start | bytes 12296 | tf_op jit(solution)/shard_map/ppermute | solution.py:24
  149.3 5.8 %collective-permute-start.21 = (f32[1,8,128]{2,1,0:T(8,128)S(1)}, f32[1,8,128]{2,1,0:T(8,128)S(1)}, u32[]{:S(2)}, u32[]{:S(2)}) collective-permute-start(f32[1,8,128]{2,1,0:T(8,128)S(1)} %fusion.117), channel_id=1, source_target_pairs={{1,0},{2,1},{3,2},{4,3},{5,4},{6,5},{7,6},{8,7},{9,8},{10,9},{11,1... | collective-permute-start | bytes 12296 | tf_op jit(solution)/shard_map/ppermute | solution.py:24
  158.5 5.8 %collective-permute-start.23 = (f32[1,8,128]{2,1,0:T(8,128)S(1)}, f32[1,8,128]{2,1,0:T(8,128)S(1)}, u32[]{:S(2)}, u32[]{:S(2)}) collective-permute-start(f32[1,8,128]{2,1,0:T(8,128)S(1)} %fusion.120), channel_id=1, source_target_pairs={{1,0},{2,1},{3,2},{4,3},{5,4},{6,5},{7,6},{8,7},{9,8},{10,9},{11,1... | collective-permute-start | bytes 12296 | tf_op jit(solution)/shard_map/ppermute | solution.py:24
  167.9 5.8 %collective-permute-start.25 = (f32[1,16,256]{2,1,0:T(8,128)S(1)}, f32[1,16,256]{2,1,0:T(8,128)S(1)}, u32[]{:S(2)}, u32[]{:S(2)}) collective-permute-start(f32[1,16,256]{2,1,0:T(8,128)S(1)} %get-tuple-element.45), channel_id=1, source_target_pairs={{1,0},{2,1},{3,2},{4,3},{5,4},{6,5},{7,6},{8,7},{9,8},{10,9},{11,1... | collective-permute-start | bytes 49160 | tf_op jit(solution)/shard_map/ppermute | solution.py:24
  177.2 5.9 %collective-permute-start.27 = (f32[1,16,256]{2,1,0:T(8,128)S(1)}, f32[1,16,256]{2,1,0:T(8,128)S(1)}, u32[]{:S(2)}, u32[]{:S(2)}) collective-permute-start(f32[1,16,256]{2,1,0:T(8,128)S(1)} %get-tuple-element.41), channel_id=1, source_target_pairs={{1,0},{2,1},{3,2},{4,3},{5,4},{6,5},{7,6},{8,7},{9,8},{10,9},{11,1... | collective-permute-start | bytes 49160 | tf_op jit(solution)/shard_map/ppermute | solution.py:24
  187.8 5.8 %collective-permute-start.29 = (f32[1,32,512]{1,2,0:T(8,128)S(1)}, f32[1,32,512]{1,2,0:T(8,128)S(1)}, u32[]{:S(2)}, u32[]{:S(2)}) collective-permute-start(f32[1,32,512]{1,2,0:T(8,128)S(1)} %get-tuple-element.17), channel_id=1, source_target_pairs={{1,0},{2,1},{3,2},{4,3},{5,4},{6,5},{7,6},{8,7},{9,8},{10,9},{11,1... | collective-permute-start | bytes 196616 | tf_op jit(solution)/shard_map/ppermute | solution.py:24
  201.5 5.9 %collective-permute-start.31 = (f32[1,32,512]{1,2,0:T(8,128)S(1)}, f32[1,32,512]{1,2,0:T(8,128)S(1)}, u32[]{:S(2)}, u32[]{:S(2)}) collective-permute-start(f32[1,32,512]{1,2,0:T(8,128)S(1)} %get-tuple-element.13), channel_id=1, source_target_pairs={{1,0},{2,1},{3,2},{4,3},{5,4},{6,5},{7,6},{8,7},{9,8},{10,9},{11,1... | collective-permute-start | bytes 196616 | tf_op jit(solution)/shard_map/ppermute | solution.py:24
  214.9 5.9 %collective-permute-start.32 = (f32[2,1,32,512]{3,2,1,0:T(8,128)S(1)}, f32[2,1,32,512]{3,2,1,0:T(8,128)S(1)}, u32[]{:S(2)}, u32[]{:S(2)}) collective-permute-start(f32[2,1,32,512]{3,2,1,0:T(8,128)S(1)} %get-tuple-element.28), channel_id=1, source_target_pairs={{1,0},{2,1},{3,2},{4,3},{5,4},{6,5},{7,6},{8,7},{9,8},{10,9},{11,1... | collective-permute-start | bytes 393224 | tf_op jit(solution)/shard_map/ppermute | solution.py:24
  223.8 5.4 %collective-permute-done.33 = f32[2,1,32,512]{3,2,1,0:T(8,128)S(1)} collective-permute-done((f32[2,1,32,512]{3,2,1,0:T(8,128)S(1)}, f32[2,1,32,512]{3,2,1,0:T(8,128)S(1)}, u32[]{:S(2)}, u32[]{:S(2)}) %collective-permute-start.33) | collective-permute-done | bytes 131104 | tf_op jit(solution)/shard_map/ppermute | solution.py:21
  231.6 39.6 %reduce-scatter.4.cloned.1.call-done = f32[64,4]{1,0:T(8,128)} async-done(((f32[512,4]{1,0:T(8,128)}), f32[64,4]{1,0:T(8,128)}) %reduce-scatter.4.cloned.1.call-update) | async-done | bytes 1040
  (165 shorter events, 87.3 us)
Async XLA Ops:
  7.2 264.0 %reduce-scatter.4.cloned.1.call-start = ((), (), s32[]{:S(2)}) async-start(), calls=%async_computation.1 | async-start | bytes 294912
  7.9 11.3 %collective-permute-start = (f32[4,512]{1,0:T(4,128)S(1)}, f32[4,512]{1,0:T(4,128)S(1)}, u32[]{:S(2)}, u32[]{:S(2)}) collective-permute-start(f32[4,512]{1,0:T(4,128)S(1)} %broadcast_subtract_fusion), channel_id=1, source_target_pairs={{0,1},{1,2},{2,3},{3,4},{4,5},{5,6},{6,7},{7,8},{8,9},{9,10},{10,1... | collective-permute-start | bytes 24584 | tf_op jit(solution)/shard_map/ppermute | solution.py:21
  9.8 9.4 %collective-permute-start.1 = (f32[4,512]{1,0:T(4,128)S(1)}, f32[4,512]{1,0:T(4,128)S(1)}, u32[]{:S(2)}, u32[]{:S(2)}) collective-permute-start(f32[4,512]{1,0:T(4,128)S(1)} %broadcast_subtract_fusion), channel_id=1, source_target_pairs={{1,0},{2,1},{3,2},{4,3},{5,4},{6,5},{7,6},{8,7},{9,8},{10,9},{11,1... | collective-permute-start | bytes 24584 | tf_op jit(solution)/shard_map/ppermute | solution.py:24
  27.4 9.8 %collective-permute-start.2 = (f32[1,32,512]{1,2,0:T(8,128)S(1)}, f32[1,32,512]{1,2,0:T(8,128)S(1)}, u32[]{:S(2)}, u32[]{:S(2)}) collective-permute-start(f32[1,32,512]{1,2,0:T(8,128)S(1)} %get-tuple-element.24), channel_id=1, source_target_pairs={{0,1},{1,2},{2,3},{3,4},{4,5},{5,6},{6,7},{7,8},{8,9},{9,10},{10,1... | collective-permute-start | bytes 196616 | tf_op jit(solution)/shard_map/ppermute | solution.py:21
  29.3 9.6 %collective-permute-start.3 = (f32[1,32,512]{1,2,0:T(8,128)S(1)}, f32[1,32,512]{1,2,0:T(8,128)S(1)}, u32[]{:S(2)}, u32[]{:S(2)}) collective-permute-start(f32[1,32,512]{1,2,0:T(8,128)S(1)} %get-tuple-element.25), channel_id=1, source_target_pairs={{1,0},{2,1},{3,2},{4,3},{5,4},{6,5},{7,6},{8,7},{9,8},{10,9},{11,1... | collective-permute-start | bytes 196616 | tf_op jit(solution)/shard_map/ppermute | solution.py:24
  42.8 10.0 %collective-permute-start.4 = (f32[1,32,512]{1,2,0:T(8,128)S(1)}, f32[1,32,512]{1,2,0:T(8,128)S(1)}, u32[]{:S(2)}, u32[]{:S(2)}) collective-permute-start(f32[1,32,512]{1,2,0:T(8,128)S(1)} %get-tuple-element.20), channel_id=1, source_target_pairs={{0,1},{1,2},{2,3},{3,4},{4,5},{5,6},{6,7},{7,8},{8,9},{9,10},{10,1... | collective-permute-start | bytes 196616 | tf_op jit(solution)/shard_map/ppermute | solution.py:21
  44.7 9.8 %collective-permute-start.5 = (f32[1,32,512]{1,2,0:T(8,128)S(1)}, f32[1,32,512]{1,2,0:T(8,128)S(1)}, u32[]{:S(2)}, u32[]{:S(2)}) collective-permute-start(f32[1,32,512]{1,2,0:T(8,128)S(1)} %get-tuple-element.21), channel_id=1, source_target_pairs={{1,0},{2,1},{3,2},{4,3},{5,4},{6,5},{7,6},{8,7},{9,8},{10,9},{11,1... | collective-permute-start | bytes 196616 | tf_op jit(solution)/shard_map/ppermute | solution.py:24
  81.8 7.9 %collective-permute-start.6 = (f32[1,16,256]{2,1,0:T(8,128)S(1)}, f32[1,16,256]{2,1,0:T(8,128)S(1)}, u32[]{:S(2)}, u32[]{:S(2)}) collective-permute-start(f32[1,16,256]{2,1,0:T(8,128)S(1)} %get-tuple-element.52), channel_id=1, source_target_pairs={{0,1},{1,2},{2,3},{3,4},{4,5},{5,6},{6,7},{7,8},{8,9},{9,10},{10,1... | collective-permute-start | bytes 49160 | tf_op jit(solution)/shard_map/ppermute | solution.py:21
  91.2 7.7 %collective-permute-start.8 = (f32[1,16,256]{2,1,0:T(8,128)S(1)}, f32[1,16,256]{2,1,0:T(8,128)S(1)}, u32[]{:S(2)}, u32[]{:S(2)}) collective-permute-start(f32[1,16,256]{2,1,0:T(8,128)S(1)} %get-tuple-element.48), channel_id=1, source_target_pairs={{0,1},{1,2},{2,3},{3,4},{4,5},{5,6},{6,7},{7,8},{8,9},{9,10},{10,1... | collective-permute-start | bytes 49160 | tf_op jit(solution)/shard_map/ppermute | solution.py:21
  101.7 7.8 %collective-permute-start.10 = (f32[1,8,128]{2,1,0:T(8,128)S(1)}, f32[1,8,128]{2,1,0:T(8,128)S(1)}, u32[]{:S(2)}, u32[]{:S(2)}) collective-permute-start(f32[1,8,128]{2,1,0:T(8,128)S(1)} %fusion.102), channel_id=1, source_target_pairs={{0,1},{1,2},{2,3},{3,4},{4,5},{5,6},{6,7},{7,8},{8,9},{9,10},{10,1... | collective-permute-start | bytes 12296 | tf_op jit(solution)/shard_map/ppermute | solution.py:21
  110.9 7.7 %collective-permute-start.12 = (f32[1,8,128]{2,1,0:T(8,128)S(1)}, f32[1,8,128]{2,1,0:T(8,128)S(1)}, u32[]{:S(2)}, u32[]{:S(2)}) collective-permute-start(f32[1,8,128]{2,1,0:T(8,128)S(1)} %fusion.105), channel_id=1, source_target_pairs={{0,1},{1,2},{2,3},{3,4},{4,5},{5,6},{6,7},{7,8},{8,9},{9,10},{10,1... | collective-permute-start | bytes 12296 | tf_op jit(solution)/shard_map/ppermute | solution.py:21
  120.0 7.7 %collective-permute-start.14 = (f32[1,8,128]{2,1,0:T(8,128)S(1)}, f32[1,8,128]{2,1,0:T(8,128)S(1)}, u32[]{:S(2)}, u32[]{:S(2)}) collective-permute-start(f32[1,8,128]{2,1,0:T(8,128)S(1)} %fusion.108), channel_id=1, source_target_pairs={{0,1},{1,2},{2,3},{3,4},{4,5},{5,6},{6,7},{7,8},{8,9},{9,10},{10,1... | collective-permute-start | bytes 12296 | tf_op jit(solution)/shard_map/ppermute | solution.py:21
  129.1 7.7 %collective-permute-start.16 = (f32[1,8,128]{2,1,0:T(8,128)S(1)}, f32[1,8,128]{2,1,0:T(8,128)S(1)}, u32[]{:S(2)}, u32[]{:S(2)}) collective-permute-start(f32[1,8,128]{2,1,0:T(8,128)S(1)} %fusion.111), channel_id=1, source_target_pairs={{0,1},{1,2},{2,3},{3,4},{4,5},{5,6},{6,7},{7,8},{8,9},{9,10},{10,1... | collective-permute-start | bytes 12296 | tf_op jit(solution)/shard_map/ppermute | solution.py:21
  138.3 7.7 %collective-permute-start.18 = (f32[1,8,128]{2,1,0:T(8,128)S(1)}, f32[1,8,128]{2,1,0:T(8,128)S(1)}, u32[]{:S(2)}, u32[]{:S(2)}) collective-permute-start(f32[1,8,128]{2,1,0:T(8,128)S(1)} %fusion.114), channel_id=1, source_target_pairs={{0,1},{1,2},{2,3},{3,4},{4,5},{5,6},{6,7},{7,8},{8,9},{9,10},{10,1... | collective-permute-start | bytes 12296 | tf_op jit(solution)/shard_map/ppermute | solution.py:21
  147.4 7.7 %collective-permute-start.20 = (f32[1,8,128]{2,1,0:T(8,128)S(1)}, f32[1,8,128]{2,1,0:T(8,128)S(1)}, u32[]{:S(2)}, u32[]{:S(2)}) collective-permute-start(f32[1,8,128]{2,1,0:T(8,128)S(1)} %fusion.117), channel_id=1, source_target_pairs={{0,1},{1,2},{2,3},{3,4},{4,5},{5,6},{6,7},{7,8},{8,9},{9,10},{10,1... | collective-permute-start | bytes 12296 | tf_op jit(solution)/shard_map/ppermute | solution.py:21
  156.6 7.7 %collective-permute-start.22 = (f32[1,8,128]{2,1,0:T(8,128)S(1)}, f32[1,8,128]{2,1,0:T(8,128)S(1)}, u32[]{:S(2)}, u32[]{:S(2)}) collective-permute-start(f32[1,8,128]{2,1,0:T(8,128)S(1)} %fusion.120), channel_id=1, source_target_pairs={{0,1},{1,2},{2,3},{3,4},{4,5},{5,6},{6,7},{7,8},{8,9},{9,10},{10,1... | collective-permute-start | bytes 12296 | tf_op jit(solution)/shard_map/ppermute | solution.py:21
  166.0 7.7 %collective-permute-start.24 = (f32[1,16,256]{2,1,0:T(8,128)S(1)}, f32[1,16,256]{2,1,0:T(8,128)S(1)}, u32[]{:S(2)}, u32[]{:S(2)}) collective-permute-start(f32[1,16,256]{2,1,0:T(8,128)S(1)} %get-tuple-element.44), channel_id=1, source_target_pairs={{0,1},{1,2},{2,3},{3,4},{4,5},{5,6},{6,7},{7,8},{8,9},{9,10},{10,1... | collective-permute-start | bytes 49160 | tf_op jit(solution)/shard_map/ppermute | solution.py:21
  175.3 7.9 %collective-permute-start.26 = (f32[1,16,256]{2,1,0:T(8,128)S(1)}, f32[1,16,256]{2,1,0:T(8,128)S(1)}, u32[]{:S(2)}, u32[]{:S(2)}) collective-permute-start(f32[1,16,256]{2,1,0:T(8,128)S(1)} %get-tuple-element.40), channel_id=1, source_target_pairs={{0,1},{1,2},{2,3},{3,4},{4,5},{5,6},{6,7},{7,8},{8,9},{9,10},{10,1... | collective-permute-start | bytes 49160 | tf_op jit(solution)/shard_map/ppermute | solution.py:21
  185.7 9.9 %collective-permute-start.28 = (f32[1,32,512]{1,2,0:T(8,128)S(1)}, f32[1,32,512]{1,2,0:T(8,128)S(1)}, u32[]{:S(2)}, u32[]{:S(2)}) collective-permute-start(f32[1,32,512]{1,2,0:T(8,128)S(1)} %get-tuple-element.16), channel_id=1, source_target_pairs={{0,1},{1,2},{2,3},{3,4},{4,5},{5,6},{6,7},{7,8},{8,9},{9,10},{10,1... | collective-permute-start | bytes 196616 | tf_op jit(solution)/shard_map/ppermute | solution.py:21
  187.8 9.6 %collective-permute-start.29 = (f32[1,32,512]{1,2,0:T(8,128)S(1)}, f32[1,32,512]{1,2,0:T(8,128)S(1)}, u32[]{:S(2)}, u32[]{:S(2)}) collective-permute-start(f32[1,32,512]{1,2,0:T(8,128)S(1)} %get-tuple-element.17), channel_id=1, source_target_pairs={{1,0},{2,1},{3,2},{4,3},{5,4},{6,5},{7,6},{8,7},{9,8},{10,9},{11,1... | collective-permute-start | bytes 196616 | tf_op jit(solution)/shard_map/ppermute | solution.py:24
  199.6 10.0 %collective-permute-start.30 = (f32[1,32,512]{1,2,0:T(8,128)S(1)}, f32[1,32,512]{1,2,0:T(8,128)S(1)}, u32[]{:S(2)}, u32[]{:S(2)}) collective-permute-start(f32[1,32,512]{1,2,0:T(8,128)S(1)} %get-tuple-element.12), channel_id=1, source_target_pairs={{0,1},{1,2},{2,3},{3,4},{4,5},{5,6},{6,7},{7,8},{8,9},{9,10},{10,1... | collective-permute-start | bytes 196616 | tf_op jit(solution)/shard_map/ppermute | solution.py:21
  201.5 9.8 %collective-permute-start.31 = (f32[1,32,512]{1,2,0:T(8,128)S(1)}, f32[1,32,512]{1,2,0:T(8,128)S(1)}, u32[]{:S(2)}, u32[]{:S(2)}) collective-permute-start(f32[1,32,512]{1,2,0:T(8,128)S(1)} %get-tuple-element.13), channel_id=1, source_target_pairs={{1,0},{2,1},{3,2},{4,3},{5,4},{6,5},{7,6},{8,7},{9,8},{10,9},{11,1... | collective-permute-start | bytes 196616 | tf_op jit(solution)/shard_map/ppermute | solution.py:24
  214.9 8.9 %collective-permute-start.32 = (f32[2,1,32,512]{3,2,1,0:T(8,128)S(1)}, f32[2,1,32,512]{3,2,1,0:T(8,128)S(1)}, u32[]{:S(2)}, u32[]{:S(2)}) collective-permute-start(f32[2,1,32,512]{3,2,1,0:T(8,128)S(1)} %get-tuple-element.28), channel_id=1, source_target_pairs={{1,0},{2,1},{3,2},{4,3},{5,4},{6,5},{7,6},{8,7},{9,8},{10,9},{11,1... | collective-permute-start | bytes 393224 | tf_op jit(solution)/shard_map/ppermute | solution.py:24
  220.9 8.4 %collective-permute-start.33 = (f32[2,1,32,512]{3,2,1,0:T(8,128)S(1)}, f32[2,1,32,512]{3,2,1,0:T(8,128)S(1)}, u32[]{:S(2)}, u32[]{:S(2)}) collective-permute-start(f32[2,1,32,512]{3,2,1,0:T(8,128)S(1)} %get-tuple-element.29), channel_id=1, source_target_pairs={{0,1},{1,2},{2,3},{3,4},{4,5},{5,6},{6,7},{7,8},{8,9},{9,10},{10,1... | collective-permute-start | bytes 393224 | tf_op jit(solution)/shard_map/ppermute | solution.py:21
  (14 other events, 133.9 us)
Sparse Core Ops, SparseCore 0:
  231.7 39.4 reduce-scatter.3
where the time goes:
time: 281 us; the launch traced here: 279 us
  starting transfers between devices  131 us (47%)
  waiting for transfers between devices  73.7 us (26%)
  local copies, waits for them, and re-layouts  32.4 us (12%)
  other arithmetic  27 us (10%)
  between operations  14.9 us (5%)
    ppermute x17, starting transfers between devices, padded(): lax.ppermute(lax.slice_in_dim(block, 0, width, axis=dim), axis, backward)  98.6 us
    unnamed x2, waiting for transfers between devices  39.6 us
    ppermute x17, starting transfers between devices, padded(): lax.ppermute(lax.slice_in_dim(block, block.shape[dim] - width, None, axis...  32.7 us
    ppermute x17, waiting for transfers between devices, padded(): lax.ppermute(lax.slice_in_dim(block, 0, width, axis=dim), axis, backward)  21.4 us
    reshape x1, local copies, waits for them, and re-layouts, restrict(): fine_values.reshape(extent[0] // 2, 2, extent[1] // 2, 2, extent[2] // 2, 2)  18.1 us
    ppermute x17, waiting for transfers between devices, padded(): lax.ppermute(lax.slice_in_dim(block, block.shape[dim] - width, None, axis...  12.8 us
    add x13, other arithmetic, jacobi(): return estimate[1:-1] + damping * (forcing - applied) / diagonal  7.86 us
    reduce_sum x3, other arithmetic, restrict(): fine_values.reshape(extent[0] // 2, 2, extent[1] // 2, 2, extent[2] // 2, 2)  7.27 us
  transfers between devices with their start and end apart: 35, of which 21 were waited for; matrix products, arithmetic and copies ran while one was open for 2% of the time, Pallas kernels for 0%

commit v1 on v0

v1 whole, which is shorter than its diff:
```python
import functools

import jax
import jax.numpy as jnp
from jax import lax
from jax.experimental import pallas as pl
from jax.experimental.pallas import tpu as pltpu
from jax.sharding import PartitionSpec as P

MESH = pl.DeviceIdType.MESH
DAMPING = 0.7
ANISOTROPY = 4.0
CEILING = 1.5
REACH = 9
C, CW, CE, CS, CN, CZ, RHO, SIG, DINV = range(9)
GW, GE, GS, GN, GZ = range(9, 14)


def iota(shape, dim):
    return lax.broadcasted_iota(jnp.int32, shape, dim)


def spread_lanes(cols):
    shape = cols[0].shape
    lane = iota(shape, 1)
    block, inner = lane >> 5, lane & 31
    turned = [
        jnp.take_along_axis(col, 4 * inner + ((block - c) & 3), axis=1, mode="promise_in_bounds")
        for c, col in enumerate(cols)
    ]
    out = []
    for p in range(4):
        mixed = turned[(3 - p) % 4]
        for b in range(3):
            mixed = jnp.where(block == b, turned[(b - p) % 4], mixed)
        out.append(mixed if p == 0 else pltpu.roll(mixed, 128 - 32 * p, 1))
    return out


def join_lanes(classes):
    shape = classes[0].shape
    lane = iota(shape, 1)
    block = lane >> 5
    turned = [cl if p == 0 else pltpu.roll(cl, 32 * p, 1) for p, cl in enumerate(classes)]
    out = []
    for c in range(4):
        mixed = turned[(3 - c) % 4]
        for b in range(3):
            mixed = jnp.where(block == b, turned[(b - c) % 4], mixed)
        source = (((lane + c) & 3) << 5) + (lane >> 2)
        out.append(jnp.take_along_axis(mixed, source, axis=1, mode="promise_in_bounds"))
    return out


def harmonic(a, b, scale):
    return scale * 2.0 * a * b / (a + b)


def level_weights(mid, west, east, open_west, open_east, scale):
    count = len(mid)
    lane = iota(mid[0].shape, 1)
    w_west = [jnp.where(open_west, harmonic(a, b, scale), 0.0) for a, b in zip(mid, west)]
    w_east = [jnp.where(open_east, harmonic(a, b, scale), 0.0) for a, b in zip(mid, east)]
    w_north = [harmonic(mid[p], mid[p + 1], scale) for p in range(count - 1)]
    last = harmonic(mid[count - 1], pltpu.roll(mid[0], 127, 1), scale)
    w_north.append(jnp.where(lane < 127, last, 0.0))
    w_south = [pltpu.roll(w_north[count - 1], 1, 1)] + w_north[:-1]
    out = []
    for p in range(count):
        w_z = (scale * ANISOTROPY) / mid[p]
        low = w_west[p] + w_east[p] + w_south[p] + w_north[p] + w_z
        full = low + w_z
        c = DAMPING / full
        out.append(
            (c, c * w_west[p], c * w_east[p], c * w_south[p], c * w_north[p], c * w_z, full / low, low / full, full / DAMPING)
        )
    return out


def terrain_weights(mid, west, east, open_west, open_east):
    lane = iota(mid[0].shape, 1)

    def share(own, other):
        both = own + other
        return 2.0 * other * other / (both * both)

    out = []
    for p in range(4):
        south = mid[p - 1] if p else pltpu.roll(mid[3], 1, 1)
        north = mid[p + 1] if p < 3 else pltpu.roll(mid[0], 127, 1)
        g_south, g_north = share(mid[p], south), share(mid[p], north)
        out.append(
            (
                jnp.where(open_west, share(mid[p], west[p]), 0.0),
                jnp.where(open_east, share(mid[p], east[p]), 0.0),
                g_south if p else jnp.where(lane > 0, g_south, 0.0),
                g_north if p < 3 else jnp.where(lane < 127, g_north, 0.0),
                -ANISOTROPY / (mid[p] * mid[p]),
            )
        )
    return out


def north_of(v, q, p):
    return v[q][p + 1] if p + 1 < len(v[q]) else pltpu.roll(v[q][0], 127, 1)


def south_of(v, q, p):
    return v[q][p - 1] if p else pltpu.roll(v[q][-1], 1, 1)


def above(v, q, p, top):
    return v[q + 1][p] if q + 1 < len(v) else jnp.where(top, 0.0, pltpu.roll(v[0][p], 7, 0))


def below(v, q, p, bottom):
    return v[q - 1][p] if q else jnp.where(bottom, 0.0, pltpu.roll(v[-1][p], 1, 0))


def around(v, v_west, v_east, w, bottom, top):
    out = []
    for q in range(len(v)):
        line = []
        for p in range(len(v[q])):
            total = w(CZ, p) * (above(v, q, p, top) + below(v, q, p, bottom))
            total = total + w(CS, p) * south_of(v, q, p) + w(CN, p) * north_of(v, q, p)
            if v_west is not None:
                total = total + w(CW, p) * v_west[q][p]
            if v_east is not None:
                total = total + w(CE, p) * v_east[q][p]
            line.append(total)
        out.append(line)
    return out


def swept(v, v_west, v_east, start, w, bottom, top):
    near = around(v, v_west, v_east, w, bottom, top)
    out = []
    for q in range(len(v)):
        line = []
        for p in range(len(v[q])):
            move = near[q][p] if q else near[q][p] * jnp.where(bottom, w(RHO, p), 1.0)
            line.append((1.0 - DAMPING) * v[q][p] + start[q][p] + move)
        out.append(line)
    return out


def restricted(v, v_west, v_east, start, w, bottom, top):
    near = around(v, v_west, v_east, w, bottom, top)
    half = len(v) // 2
    out = [[0.0] * half for _ in range(half)]
    for q1 in range(half):
        for p in range(len(v)):
            part = 0.0
            for q in (2 * q1, 2 * q1 + 1):
                own = -DAMPING * v[q][p] if start is None else start[q][p] - DAMPING * v[q][p]
                if q == 0:
                    own = own * jnp.where(bottom, w(SIG, p), 1.0)
                part = part + (near[q][p] + own)
            out[q1][p // 2] = out[q1][p // 2] + w(DINV, p) * part
    return out


def edge_restricted(v, kind, w):
    half = len(v) // 2
    return [
        [sum((w(DINV, p) * w(kind, p)) * (v[2 * q1][p] + v[2 * q1 + 1][p]) for p in (2 * p1, 2 * p1 + 1)) for p1 in range(half)]
        for q1 in range(half)
    ]


def edge_swept(v, kind, w, bottom):
    return [
        [w(kind, p) * (v[q][p] if q else v[q][p] * jnp.where(bottom, w(RHO, p), 1.0)) for p in range(len(v[q]))]
        for q in range(len(v))
    ]


def added(a, b):
    return [[s + t for s, t in zip(x, y)] for x, y in zip(a, b)]


def first_guess(f, w, bottom):
    return [
        [w(C, p) * (f[q][p] if q else f[q][p] * jnp.where(bottom, w(RHO, p), 1.0)) for p in range(len(f[q]))]
        for q in range(len(f))
    ]


def grid_of(block, count):
    return [[block[q * count + p] for p in range(count)] for q in range(count)]


def table(ref, row):
    @functools.cache
    def weight(kind, p):
        return ref[kind, p, pl.ds(row, 1), :]

    return weight


def put_row(ref, row, tiles):
    count = len(tiles)
    for q in range(count):
        for p in range(count):
            ref[row, q * count + p] = tiles[q][p]


def kernel(
    n_dir, n_gx,
    cot, pot, height, adjoint, gradient,
    h_in, c_in, p_in, a_out, mixed,
    hs, fs, ps, ds, w0, de, d1, w1, df, d2s, d2, w2,
    v0, v1, v2, v3,
    f1p, f1e, f2p, f2e, f2own, f2r, f1, u0, u1, u2, u3,
    gn, er,
    local_sem, send_sem, recv_sem,
):
    me_dir, me = lax.axis_index("dir"), lax.axis_index("gx")

    def strip(offset):
        return {"gx": lax.rem(me + offset + REACH * n_gx, n_gx)}

    barrier = pltpu.get_barrier_semaphore()
    reach = [o for o in range(-REACH, REACH + 1) if o]
    for offset in reach:
        pl.semaphore_signal(barrier, inc=1, device_id=strip(offset), device_id_type=MESH)
    for step in range(1, n_dir):
        pl.semaphore_signal(
            barrier, inc=1, device_id={"dir": lax.rem(me_dir + step, n_dir)}, device_id_type=MESH
        )

    height_in = pltpu.make_async_copy(height, h_in, local_sem.at[0])
    cot_in = pltpu.make_async_copy(cot.at[0], c_in, local_sem.at[1])
    pot_in = pltpu.make_async_copy(pot.at[0], p_in, local_sem.at[2])
    height_in.start()
    cot_in.start()
    pot_in.start()

    sent = []

    def send(source, target, device):
        index = len(sent)
        copy = pltpu.make_async_remote_copy(
            src_ref=source, dst_ref=target, send_sem=send_sem.at[index], recv_sem=recv_sem.at[index],
            device_id=device, device_id_type=MESH,
        )
        copy.start()
        sent.append(copy)
        return copy

    bottom, top = iota((8, 128), 0) == 0, iota((8, 128), 0) == 7

    for p in range(4):
        ds[p, 24:32, :] = jnp.ones((8, 128), jnp.float32)
    d2[...] = jnp.ones(d2.shape, jnp.float32)
    d1[...] = jnp.ones(d1.shape, jnp.float32)

    height_in.wait()
    raw = h_in[...]
    for p, cl in enumerate(spread_lanes([raw[:, 128 * c : 128 * c + 128] for c in range(4)])):
        hs[3, 4 * p : 4 * p + 4, :] = CEILING - cl

    pl.semaphore_wait(barrier, len(reach) + n_dir - 1)
    depth_copies = [send(hs.at[3], hs.at[3 - o], strip(o)) for o in (-1, 1, -2, 2, -3, 3)]

    def spread_row(source, target, row, slot):
        block = source[row]
        for p, cl in enumerate(spread_lanes([block[:, 128 * c : 128 * c + 128] for c in range(4)])):
            target[slot, p] = cl

    cot_in.wait()
    for x in range(0, 4):
        spread_row(c_in, fs, x, x + 4)
    field_copies = [
        send(fs.at[pl.ds(4, 4)], fs.at[pl.ds(4 - 4 * o, 4)], strip(o)) for o in (-1, 1)
    ]

    def field_row(ref, slot):
        return [[ref[slot, p, pl.ds(q, 8, stride=4), :] for p in range(4)] for q in range(4)]

    for copy in depth_copies:
        copy.wait_recv()
    for o in range(7):
        for p in range(4):
            ds[p, 4 * o : 4 * o + 4, :] = hs[o, 4 * p : 4 * p + 4, :]
    for p1 in range(2):
        de[p1] = ds[2 * p1] + ds[2 * p1 + 1]
    for p1 in range(2):
        d1[p1, 0:16, :] = 0.25 * (de[p1, pl.ds(0, 16, stride=2), :] + de[p1, pl.ds(1, 16, stride=2), :])
    df[...] = d1[0] + d1[1]
    d2s[1] = 0.25 * (df[pl.ds(0, 8, stride=2), :] + df[pl.ds(1, 8, stride=2), :])
    d2_copies = [send(d2s.at[1], d2s.at[1 - s], strip(7 * s)) for s in (-1, 1)]

    def faces(rows, per_strip, first):
        size = n_gx * per_strip
        place = (me * per_strip + first + REACH * size + iota((rows, 128), 0)) & (size - 1)
        return place != 0, place != size - 1

    open_west, open_east = faces(16, 4, -4)
    mid = [ds[p, 8:24, :] for p in range(4)]
    west = [ds[p, 7:23, :] for p in range(4)]
    east = [ds[p, 9:25, :] for p in range(4)]
    for p, kinds in enumerate(level_weights(mid, west, east, open_west, open_east, 1.0)):
        for kind, value in enumerate(kinds):
            w0[kind, p] = value
    open_west, open_east = faces(16, 2, -5)
    mid1 = [d1[p, 1:17, :] for p in range(2)]
    west1 = [d1[p, 0:16, :] for p in range(2)]
    east1 = [d1[p, 2:18, :] for p in range(2)]
    for p, kinds in enumerate(level_weights(mid1, west1, east1, open_west, open_east, 2.0)):
        for kind, value in enumerate(kinds):
            w1[kind, p] = value

    def guess_row(i):
        put_row(v0, i, first_guess(field_row(fs, i), table(w0, i), bottom))

    def row_of(ref, i, count=4):
        return grid_of(ref[i], count)

    def smooth_rows(source, target, low, high):
        have = {i: row_of(source, i) for i in range(low - 1, high + 1)}
        for i in range(low, high):
            put_row(target, i, swept(have[i], have[i - 1], have[i + 1], row_of(v0, i), table(w0, i), bottom, top))

    for i in range(4, 8):
        guess_row(i)
    have = [None] + [row_of(v0, i) for i in range(4, 8)] + [None]
    put_row(v1, 3, edge_swept(have[1], CE, table(w0, 3), bottom))
    for i in range(4, 8):
        put_row(v1, i, swept(have[i - 3], have[i - 4], have[i - 2], have[i - 3], table(w0, i), bottom, top))
    put_row(v1, 8, edge_swept(have[4], CW, table(w0, 8), bottom))
    have = [None] + [row_of(v1, i) for i in range(3, 9)] + [None]
    rest = {i: restricted(have[i - 2], have[i - 3], have[i - 1], row_of(v0, i) if 4 <= i <= 7 else None, table(w0, i), bottom, top) for i in range(3, 9)}
    rest[2] = edge_restricted(have[1], CE, table(w0, 2))
    rest[9] = edge_restricted(have[6], CW, table(w0, 9))
    for i in range(4):
        put_row(f1p, i, added(rest[2 * i + 2], rest[2 * i + 3]))

    begin = {i: first_guess(grid_of(f1p[i - 4], 2), table(w1, i), bottom) for i in range(4, 8)}
    next_row = {i: swept(begin[i], begin.get(i - 1), begin.get(i + 1), begin[i], table(w1, i), bottom, top) for i in range(4, 8)}
    next_row[3] = edge_swept(begin[4], CE, table(w1, 3), bottom)
    next_row[8] = edge_swept(begin[7], CW, table(w1, 8), bottom)
    rest = {
        i: restricted(next_row[i], next_row.get(i - 1), next_row.get(i + 1), begin.get(i), table(w1, i), bottom, top)
        for i in range(3, 9)
    }
    rest[2] = edge_restricted(next_row[3], CE, table(w1, 2))
    rest[9] = edge_restricted(next_row[8], CW, table(w1, 9))
    for coarse, near_rows in enumerate(((2,), (3, 4), (5, 6), (7, 8), (9,))):
        f2p[coarse] = sum(rest[i][0][0] for i in near_rows)
    slot_of = {2: 0, 1: 1, -1: 2, -2: 3}
    f2_copies = [send(f2p.at[2 + o], f2e.at[slot_of[o]], strip(o)) for o in (-1, 1, -2, 2)]
    f1_copies = [send(f1p.at[0], f1e.at[1], strip(-1)), send(f1p.at[3], f1e.at[0], strip(1))]

    pot_in.wait()
    for x in range(0, 4):
        spread_row(p_in, ps, x, x + 1)
    potential_copies = [send(ps.at[1], ps.at[5], strip(-1)), send(ps.at[4], ps.at[0], strip(1))]

    for copy in d2_copies:
        copy.wait_recv()
    d2[0:8, :] = d2s[0]
    d2[7:15, :] = d2s[1]
    d2[14:22, :] = d2s[2]
    open_west, open_east = faces(24, 1, -9)
    for kind, value in enumerate(
        level_weights([d2[1:25, :]], [d2[0:24, :]], [d2[2:26, :]], open_west, open_east, 4.0)[0]
    ):
        w2[kind, 0] = value

    for copy in f2_copies:
        copy.wait_recv()
    f2own[0] = f2p[2] + ((f2e[0] + f2e[1]) + (f2e[2] + f2e[3]))
    place_of = {o: (o + REACH if o < 0 else o + REACH - 1) for o in reach}
    row_copies = [send(f2own.at[0], f2r.at[place_of[-o]], strip(o)) for s in range(1, REACH + 1) for o in (-s, s)]
    for copy in f1_copies:
        copy.wait_recv()
    f1[6] = f1p[1] + f1e[0]
    f1[7] = f1p[2] + f1e[1]
    f1_copies = [
        send(f1.at[pl.ds(6, 2)], f1.at[pl.ds(6 - 2 * o, 2)], strip(o)) for o in (-1, 1, -2, 2, -3, 3)
    ]

    terrain = terrain_weights(
        [ds[p, 8:24, :] for p in range(4)], [ds[p, 7:23, :] for p in range(4)], [ds[p, 9:25, :] for p in range(4)],
        *faces(16, 4, -4),
    )
    for p, kinds in enumerate(terrain):
        for kind, value in enumerate(kinds):
            w0[GW + kind, p] = value
    for copy in field_copies:
        copy.wait_recv()
    for i in range(0, 4):
        guess_row(i)
    for i in range(8, 12):
        guess_row(i)
    smooth_rows(v0, v1, 1, 11)

    for copy in f1_copies:
        copy.wait_recv()
    for i in range(0, 12):
        put_row(u0, i, first_guess(grid_of(f1[i + 1], 2), table(w1, i), bottom))
    for i in range(1, 11):
        rows = [row_of(u0, i + d, 2) for d in (0, -1, 1)]
        put_row(u1, i, swept(*rows, row_of(u0, i, 2), table(w1, i), bottom, top))

    for copy in row_copies:
        copy.wait_recv()
    start = []
    for o in range(-REACH, REACH + 1):
        source = f2r[place_of[o]] if o else f2own[0]
        start.append(first_guess([[source]], table(w2, o + REACH), bottom))
    now = start
    for sweep in range(7):
        later = [None] * len(now)
        for i in range(sweep + 1, len(now) - sweep - 1):
            later[i] = swept(now[i], now[i - 1], now[i + 1], start[i], table(w2, i), bottom, top)
        now = later

    for i in range(1, 11):
        fix = now[(i - 5) // 2 + REACH][0][0]
        put_row(u1, i, [[t + fix for t in line] for line in row_of(u1, i, 2)])
    for source, target, low, high in ((u1, u2, 2, 10), (u2, u3, 3, 9)):
        for i in range(low, high):
            rows = [row_of(source, i + d, 2) for d in (0, -1, 1)]
            put_row(target, i, swept(*rows, row_of(u0, i, 2), table(w1, i), bottom, top))

    def corrected_row(i):
        fix = row_of(u3, (i - 4 + 8) // 2 + 1, 2)
        now_row = row_of(v1, i)
        put_row(v1, i, [[now_row[q][p] + fix[q // 2][p // 2] for p in range(4)] for q in range(4)])

    for i in range(1, 11):
        corrected_row(i)
    smooth_rows(v1, v2, 2, 10)
    smooth_rows(v2, v3, 3, 9)

    for copy in potential_copies:
        copy.wait_recv()

    def terrain_row(x):
        w = table(w0, x + 4)
        a, a_west, a_east = (row_of(v3, x + 4 + d) for d in (0, -1, 1))
        b, b_west, b_east = (field_row(ps, x + 1 + d) for d in (0, -1, 1))
        zeros = jnp.zeros((8, 128), jnp.float32)
        by_z, by_west, by_east, by_north = ([zeros] * 4 for _ in range(4))
        for q in range(4):
            for p in range(4):
                by_z[p] += (above(a, q, p, top) - a[q][p]) * (above(b, q, p, top) - b[q][p])
                by_west[p] += (a[q][p] - a_west[q][p]) * (b[q][p] - b_west[q][p])
                by_east[p] += (a_east[q][p] - a[q][p]) * (b_east[q][p] - b[q][p])
                by_north[p] += (north_of(a, q, p) - a[q][p]) * (north_of(b, q, p) - b[q][p])
        out = []
        for p in range(4):
            by_south = by_north[p - 1] if p else pltpu.roll(by_north[3], 1, 1)
            total = w(GW, p) * by_west[p] + w(GE, p) * by_east[p] + w(GN, p) * by_north[p]
            total = total + w(GS, p) * by_south + w(GZ, p) * by_z[p]
            out.append(jnp.sum(total, axis=0, keepdims=True))
        return out

    sums = [terrain_row(x) for x in range(4)]
    blank = jnp.zeros((4, 128), jnp.float32)
    packed = [jnp.concatenate([sums[x][p] for x in range(4)] + [blank], axis=0) for p in range(4)]
    for c, tile in enumerate(join_lanes(packed)):
        gn[c] = tile
    dir_copies = []
    for step in range(1, n_dir):
        target = lax.rem(me_dir + step, n_dir)
        dir_copies.append(send(gn.at[target // (n_dir // 4)], er.at[step - 1], {"dir": target}))

    def natural_row(x):
        now_row = row_of(v3, x + 4)
        for p in range(4):
            for q in range(4):
                mixed[x, p, pl.ds(q, 8, stride=4), :] = now_row[q][p]
        for c, tile in enumerate(join_lanes([mixed[x, p] for p in range(4)])):
            a_out[x, :, 128 * c : 128 * c + 128] = tile

    for i in range(0, 4):
        natural_row(i)
    out_copy = pltpu.make_async_copy(a_out, adjoint.at[0], local_sem.at[3])
    out_copy.start()

    for copy in dir_copies:
        copy.wait_recv()
    total = gn[me_dir // (n_dir // 4)]
    for step in range(1, n_dir):
        total = total + er[step - 1]
    part = lax.rem(me_dir, n_dir // 4)
    mine = total
    width = gradient.shape[1]
    for k in range(1, 128 // width):
        mine = jnp.where(iota((8, 128), 0) * 0 + part == k, pltpu.roll(total, 128 - k * width, 1), mine)
    gradient[...] = mine[0:4, 0:width]

    out_copy.wait()
    for copy in sent:
        copy.wait_send()


def body(cotangent, potential, height):
    n_dir, n_gx = lax.axis_size("dir"), lax.axis_size("gx")
    f32 = jnp.float32
    shapes = [
        (4, 512), (4, 32, 512), (4, 32, 512), (4, 32, 512), (4, 4, 32, 128),
        (7, 16, 128), (12, 4, 32, 128), (6, 4, 32, 128), (4, 32, 128), (14, 4, 16, 128),
        (2, 32, 128), (2, 24, 128), (9, 2, 16, 128), (24, 128), (3, 8, 128), (32, 128), (9, 1, 24, 128),
        (12, 16, 8, 128), (12, 16, 8, 128), (12, 16, 8, 128), (12, 16, 8, 128),
        (4, 4, 8, 128), (2, 4, 8, 128), (5, 8, 128), (4, 8, 128), (1, 8, 128), (18, 8, 128), (14, 4, 8, 128),
        (12, 4, 8, 128), (12, 4, 8, 128), (12, 4, 8, 128), (12, 4, 8, 128),
        (4, 8, 128), (n_dir - 1, 8, 128),
    ]
    copies = 6 + 2 + 2 + 4 + 2 + 2 + 2 * REACH + 6 + n_dir - 1
    return pl.pallas_call(
        functools.partial(kernel, n_dir, n_gx),
        out_shape=(
            jax.ShapeDtypeStruct(cotangent.shape, f32),
            jax.ShapeDtypeStruct((height.shape[0], height.shape[1] // n_dir), f32),
        ),
        in_specs=[pl.BlockSpec(memory_space=pltpu.HBM)] * 3,
        out_specs=(pl.BlockSpec(memory_space=pl.ANY), pl.BlockSpec(memory_space=pltpu.VMEM)),
        scratch_shapes=[pltpu.VMEM(shape, f32) for shape in shapes]
        + [pltpu.SemaphoreType.DMA((4,)), pltpu.SemaphoreType.DMA((copies,)), pltpu.SemaphoreType.DMA((copies,))],
        compiler_params=pltpu.CompilerParams(
            collective_id=0, has_side_effects=True, vmem_limit_bytes=60 * 1024 * 1024
        ),
        name="vcycle",
    )(cotangent, potential, height)


def solution(mesh):
    placed = (P("dir", "gx", None, None), P("dir", "gx", None, None), P("gx", None))
    return jax.shard_map(
        body,
        mesh=mesh,
        in_specs=placed,
        out_specs=(P("dir", "gx", None, None), P("gx", "dir")),
        check_vma=False,
    )
```

time: 281 us -> 42.1 us (0.15)
  the two profiles are of different devices: /device:TPU:6 before, /device:TPU:1 now
where the time goes in v1:
time: 42.1 us; the launch traced here: 41.9 us
  Pallas kernels  39 us (93%)
  local copies, waits for them, and re-layouts  2.25 us (5%)
  between operations  0.65 us (2%)
    pallas_call x1, Pallas kernels, body(): pl.pallas_call(functools.partial(kernel, n_dir, n_gx), out_shape=(jax.Sha...  39 us
    unnamed x4, local copies, waits for them, and re-layouts  2.25 us

profile of v1, /device:TPU:1, one launch (start us, length us, event | category | flops | bytes accessed | tf_op | source)
XLA Modules:
  0.0 41.9 jit_solution(15619647826183977703)
XLA Ops:
  0.6 39.0 %vcycle.1 = (f32[1,4,32,512]{3,2,1,0:T(8,128)}, f32[4,64]{1,0:T(4,128)}) custom-call(f32[1,4,32,512]{3,2,1,0:T(8,128)} %cot.1, f32[1,4,32,512]{3,2,1,0:T(8,128)} %pot.1, f32[4,512]{1,0:T(4,128)} %height.1), custom_call_target="tpu_custom_call" | custom-call | tf_op jit(solution)/shard_map/vcycle/pallas_call | solution.py:515
  39.7 0.0 copy-start
  39.7 1.7 %copy.7 = f32[1,4,32,512]{3,2,1,0:T(8,128)} copy(f32[1,4,32,512]{3,2,1,0:T(8,128)} %get-tuple-element.4) | data formatting | bytes 524288
  41.4 0.0 copy-done
  41.4 0.6 %copy.8 = f32[4,64]{1,0:T(4,128)} copy(f32[4,64]{1,0:T(4,128)S(1)} %copy-done) | data formatting | bytes 2048
Async XLA Ops:
  39.7 1.7 %copy-start = (f32[4,64]{1,0:T(4,128)S(1)}, f32[4,64]{1,0:T(4,128)}, u32[]{:S(2)}) copy-start(f32[4,64]{1,0:T(4,128)} %get-tuple-element.5) | copy-start | bytes 3076

commit v2 on v1

--- a/solution.py
+++ b/solution.py
@@ -12,6 +12,7 @@
 ANISOTROPY = 4.0
 CEILING = 1.5
 REACH = 9
+GREET = 4
 C, CW, CE, CS, CN, CZ, RHO, SIG, DINV = range(9)
 GW, GE, GS, GN, GZ = range(9, 14)
 
@@ -212,18 +213,18 @@
     h_in, c_in, p_in, a_out, mixed,
     hs, fs, ps, ds, w0, de, d1, w1, df, d2s, d2, w2,
     v0, v1, v2, v3,
-    f1p, f1e, f2p, f2e, f2own, f2r, f1, u0, u1, u2, u3,
+    packet, from_west, from_east, from_west2, from_east2, from_west3, from_east3, f2own, f2r, f1, u0, u1, u2, u3,
     gn, er,
     local_sem, send_sem, recv_sem,
 ):
     me_dir, me = lax.axis_index("dir"), lax.axis_index("gx")
 
     def strip(offset):
-        return {"gx": lax.rem(me + offset + REACH * n_gx, n_gx)}
+        return {"gx": lax.rem(me + offset + 9 * n_gx, n_gx)}
 
     barrier = pltpu.get_barrier_semaphore()
-    reach = [o for o in range(-REACH, REACH + 1) if o]
-    for offset in reach:
+    greeted = [o for s in range(1, GREET + 1) for o in (-s, s)]
+    for offset in greeted:
         pl.semaphore_signal(barrier, inc=1, device_id=strip(offset), device_id_type=MESH)
     for step in range(1, n_dir):
         pl.semaphore_signal(
@@ -261,7 +262,7 @@
     for p, cl in enumerate(spread_lanes([raw[:, 128 * c : 128 * c + 128] for c in range(4)])):
         hs[3, 4 * p : 4 * p + 4, :] = CEILING - cl
 
-    pl.semaphore_wait(barrier, len(reach) + n_dir - 1)
+    pl.semaphore_wait(barrier, len(greeted) + n_dir - 1)
     depth_copies = [send(hs.at[3], hs.at[3 - o], strip(o)) for o in (-1, 1, -2, 2, -3, 3)]
 
     def spread_row(source, target, row, slot):
@@ -334,10 +335,13 @@
     rest = {i: restricted(have[i - 2], have[i - 3], have[i - 1], row_of(v0, i) if 4 <= i <= 7 else None, table(w0, i), bottom, top) for i in range(3, 9)}
     rest[2] = edge_restricted(have[1], CE, table(w0, 2))
     rest[9] = edge_restricted(have[6], CW, table(w0, 9))
-    for i in range(4):
-        put_row(f1p, i, added(rest[2 * i + 2], rest[2 * i + 3]))
-
-    begin = {i: first_guess(grid_of(f1p[i - 4], 2), table(w1, i), bottom) for i in range(4, 8)}
+    f1p = [added(rest[2 * i + 2], rest[2 * i + 3]) for i in range(4)]
+    for q in range(2):
+        for p in range(2):
+            packet[2 * q + p] = f1p[0][q][p]
+            packet[9 + 2 * q + p] = f1p[3][q][p]
+
+    begin = {i: first_guess(f1p[i - 4], table(w1, i), bottom) for i in range(4, 8)}
     next_row = {i: swept(begin[i], begin.get(i - 1), begin.get(i + 1), begin[i], table(w1, i), bottom, top) for i in range(4, 8)}
     next_row[3] = edge_swept(begin[4], CE, table(w1, 3), bottom)
     next_row[8] = edge_swept(begin[7], CW, table(w1, 8), bottom)
@@ -347,11 +351,17 @@
     }
     rest[2] = edge_restricted(next_row[3], CE, table(w1, 2))
     rest[9] = edge_restricted(next_row[8], CW, table(w1, 9))
-    for coarse, near_rows in enumerate(((2,), (3, 4), (5, 6), (7, 8), (9,))):
-        f2p[coarse] = sum(rest[i][0][0] for i in near_rows)
-    slot_of = {2: 0, 1: 1, -1: 2, -2: 3}
-    f2_copies = [send(f2p.at[2 + o], f2e.at[slot_of[o]], strip(o)) for o in (-1, 1, -2, 2)]
-    f1_copies = [send(f1p.at[0], f1e.at[1], strip(-1)), send(f1p.at[3], f1e.at[0], strip(1))]
+    f2p = [sum(rest[i][0][0] for i in rows) for rows in ((2,), (3, 4), (5, 6), (7, 8), (9,))]
+    for k in range(5):
+        packet[4 + k] = f2p[k]
+    sum_copies = [
+        send(packet.at[pl.ds(0, 7)], from_east, strip(-1)),
+        send(packet.at[pl.ds(6, 7)], from_west, strip(1)),
+        send(packet.at[pl.ds(4, 2)], from_east2, strip(-2)),
+        send(packet.at[pl.ds(7, 2)], from_west2, strip(2)),
+        send(packet.at[4], from_east3.at[0], strip(-3)),
+        send(packet.at[8], from_west3.at[0], strip(3)),
+    ]
 
     pot_in.wait()
     for x in range(0, 4):
@@ -369,18 +379,19 @@
     ):
         w2[kind, 0] = value
 
-    for copy in f2_copies:
-        copy.wait_recv()
-    f2own[0] = f2p[2] + ((f2e[0] + f2e[1]) + (f2e[2] + f2e[3]))
-    place_of = {o: (o + REACH if o < 0 else o + REACH - 1) for o in reach}
-    row_copies = [send(f2own.at[0], f2r.at[place_of[-o]], strip(o)) for s in range(1, REACH + 1) for o in (-s, s)]
-    for copy in f1_copies:
-        copy.wait_recv()
-    f1[6] = f1p[1] + f1e[0]
-    f1[7] = f1p[2] + f1e[1]
-    f1_copies = [
-        send(f1.at[pl.ds(6, 2)], f1.at[pl.ds(6 - 2 * o, 2)], strip(o)) for o in (-1, 1, -2, 2, -3, 3)
-    ]
+    for copy in sum_copies:
+        copy.wait_recv()
+    f2own[0] = (f2p[1] + from_west[0]) + (from_east[4] + from_west2[0]) + from_west3[0]
+    f2own[1] = (f2p[2] + from_west[1]) + (from_east[5] + from_west2[1]) + from_east2[0]
+    f2own[2] = (f2p[3] + from_west[2]) + (from_east[6] + from_east2[1]) + from_east3[0]
+    slots = (-9, -6, -3, 3, 6, 9)
+    row_copies = [send(f2own, f2r.at[slots.index(-o)], strip(o)) for o in (-9, 9, -6, 6, -3, 3)]
+    for q in range(2):
+        for p in range(2):
+            f1[6, 2 * q + p] = f1p[1][q][p] + from_west[3 + 2 * q + p]
+            f1[7, 2 * q + p] = f1p[2][q][p] + from_east[2 * q + p]
+    f1_copies = [send(f1.at[pl.ds(6, 2)], f1.at[pl.ds(6 - 2 * o, 2)], strip(o)) for o in (-1, 1, -2, 2)]
+    f1_copies += [send(f1.at[6], f1.at[12], strip(-3)), send(f1.at[7], f1.at[1], strip(3))]
 
     terrain = terrain_weights(
         [ds[p, 8:24, :] for p in range(4)], [ds[p, 7:23, :] for p in range(4)], [ds[p, 9:25, :] for p in range(4)],
@@ -409,7 +420,8 @@
         copy.wait_recv()
     start = []
     for o in range(-REACH, REACH + 1):
-        source = f2r[place_of[o]] if o else f2own[0]
+        block = (o + 10) // 3 * 3 - 9
+        source = f2own[o + 1] if block == 0 else f2r[slots.index(block), o - block + 1]
         start.append(first_guess([[source]], table(w2, o + REACH), bottom))
     now = start
     for sweep in range(7):
@@ -507,16 +519,16 @@
         (7, 16, 128), (12, 4, 32, 128), (6, 4, 32, 128), (4, 32, 128), (14, 4, 16, 128),
         (2, 32, 128), (2, 24, 128), (9, 2, 16, 128), (24, 128), (3, 8, 128), (32, 128), (9, 1, 24, 128),
         (12, 16, 8, 128), (12, 16, 8, 128), (12, 16, 8, 128), (12, 16, 8, 128),
-        (4, 4, 8, 128), (2, 4, 8, 128), (5, 8, 128), (4, 8, 128), (1, 8, 128), (18, 8, 128), (14, 4, 8, 128),
+        (13, 8, 128), (7, 8, 128), (7, 8, 128), (2, 8, 128), (2, 8, 128), (1, 8, 128), (1, 8, 128), (3, 8, 128), (6, 3, 8, 128), (14, 4, 8, 128),
         (12, 4, 8, 128), (12, 4, 8, 128), (12, 4, 8, 128), (12, 4, 8, 128),
         (4, 8, 128), (n_dir - 1, 8, 128),
     ]
-    copies = 6 + 2 + 2 + 4 + 2 + 2 + 2 * REACH + 6 + n_dir - 1
+    copies = 6 + 2 + 2 + 2 + 6 + 6 + 6 + n_dir - 1
     return pl.pallas_call(
         functools.partial(kernel, n_dir, n_gx),
         out_shape=(
-            jax.ShapeDtypeStruct(cotangent.shape, f32),
-            jax.ShapeDtypeStruct((height.shape[0], height.shape[1] // n_dir), f32),
+            pltpu.VMEM(cotangent.shape, f32),
+            pltpu.VMEM((height.shape[0], height.shape[1] // n_dir), f32),
         ),
         in_specs=[pl.BlockSpec(memory_space=pltpu.HBM)] * 3,
         out_specs=(pl.BlockSpec(memory_space=pl.ANY), pl.BlockSpec(memory_space=pltpu.VMEM)),

time: 42.1 us -> 39.5 us (0.938)
  Pallas kernels: 39 us -> 37.4 us
  local copies, waits for them, and re-layouts: 2.25 us -> 1.28 us
    pallas_call x1, Pallas kernels: 39 us -> 37.4 us  [body(): pl.pallas_call(functools.partial(kernel, n_dir, n_gx), out_shape=(pltpu.V...]
    unnamed x4 -> x2, local copies, waits for them, and re-layouts: 2.25 us -> 1.28 us
where the time goes in v2:
time: 39.5 us; the launch traced here: 39.3 us
  Pallas kernels  37.4 us (95%)
  local copies, waits for them, and re-layouts  1.28 us (3%)
  between operations  0.64 us (2%)
    pallas_call x1, Pallas kernels, body(): pl.pallas_call(functools.partial(kernel, n_dir, n_gx), out_shape=(pltpu.V...  37.4 us
    unnamed x2, local copies, waits for them, and re-layouts  1.28 us

profile of v2, /device:TPU:1, one launch (start us, length us, event | category | flops | bytes accessed | tf_op | source)
XLA Modules:
  0.0 39.3 jit_solution(9758607762735802024)
XLA Ops:
  0.6 37.4 %vcycle.1 = (f32[1,4,32,512]{3,2,1,0:T(8,128)S(1)}, f32[4,64]{1,0:T(4,128)S(1)}) custom-call(f32[1,4,32,512]{3,2,1,0:T(8,128)} %cot.1, f32[1,4,32,512]{3,2,1,0:T(8,128)} %pot.1, f32[4,512]{1,0:T(4,128)} %height.1), custom_call_target="tpu_custom_call" | custom-call | tf_op jit(solution)/shard_map/vcycle/pallas_call | solution.py:527
  38.0 0.7 %copy.7 = f32[1,4,32,512]{3,2,1,0:T(8,128)} copy(f32[1,4,32,512]{3,2,1,0:T(8,128)S(1)} %get-tuple-element.2) | data formatting | bytes 524288
  38.7 0.6 %copy.8 = f32[4,64]{1,0:T(4,128)} copy(f32[4,64]{1,0:T(4,128)S(1)} %get-tuple-element.3) | data formatting | bytes 2048

commit v3 on v2

--- a/solution.py
+++ b/solution.py
@@ -366,7 +366,6 @@
     pot_in.wait()
     for x in range(0, 4):
         spread_row(p_in, ps, x, x + 1)
-    potential_copies = [send(ps.at[1], ps.at[5], strip(-1)), send(ps.at[4], ps.at[0], strip(1))]
 
     for copy in d2_copies:
         copy.wait_recv()
@@ -393,6 +392,8 @@
     f1_copies = [send(f1.at[pl.ds(6, 2)], f1.at[pl.ds(6 - 2 * o, 2)], strip(o)) for o in (-1, 1, -2, 2)]
     f1_copies += [send(f1.at[6], f1.at[12], strip(-3)), send(f1.at[7], f1.at[1], strip(3))]
 
+    potential_copies = [send(ps.at[1], ps.at[5], strip(-1)), send(ps.at[4], ps.at[0], strip(1))]
+
     terrain = terrain_weights(
         [ds[p, 8:24, :] for p in range(4)], [ds[p, 7:23, :] for p in range(4)], [ds[p, 9:25, :] for p in range(4)],
         *faces(16, 4, -4),
@@ -407,14 +408,6 @@
     for i in range(8, 12):
         guess_row(i)
     smooth_rows(v0, v1, 1, 11)
-
-    for copy in f1_copies:
-        copy.wait_recv()
-    for i in range(0, 12):
-        put_row(u0, i, first_guess(grid_of(f1[i + 1], 2), table(w1, i), bottom))
-    for i in range(1, 11):
-        rows = [row_of(u0, i + d, 2) for d in (0, -1, 1)]
-        put_row(u1, i, swept(*rows, row_of(u0, i, 2), table(w1, i), bottom, top))
 
     for copy in row_copies:
         copy.wait_recv()
@@ -430,6 +423,13 @@
             later[i] = swept(now[i], now[i - 1], now[i + 1], start[i], table(w2, i), bottom, top)
         now = later
 
+    for copy in f1_copies:
+        copy.wait_recv()
+    for i in range(0, 12):
+        put_row(u0, i, first_guess(grid_of(f1[i + 1], 2), table(w1, i), bottom))
+    for i in range(1, 11):
+        rows = [row_of(u0, i + d, 2) for d in (0, -1, 1)]
+        put_row(u1, i, swept(*rows, row_of(u0, i, 2), table(w1, i), bottom, top))
     for i in range(1, 11):
         fix = now[(i - 5) // 2 + REACH][0][0]
         put_row(u1, i, [[t + fix for t in line] for line in row_of(u1, i, 2)])

time: 39.5 us -> 39.5 us (level)
  no operation moved by 1% of the time
where the time goes in v3:
time: 39.5 us; the launch traced here: 39.3 us
  Pallas kernels  37.4 us (95%)
  local copies, waits for them, and re-layouts  1.28 us (3%)
  between operations  0.64 us (2%)
    pallas_call x1, Pallas kernels, body(): pl.pallas_call(functools.partial(kernel, n_dir, n_gx), out_shape=(pltpu.V...  37.4 us
    unnamed x2, local copies, waits for them, and re-layouts  1.28 us

profile of v3, /device:TPU:1, one launch (start us, length us, event | category | flops | bytes accessed | tf_op | source)
XLA Modules:
  0.0 39.3 jit_solution(9419139062403674324)
XLA Ops:
  0.6 37.4 %vcycle.1 = (f32[1,4,32,512]{3,2,1,0:T(8,128)S(1)}, f32[4,64]{1,0:T(4,128)S(1)}) custom-call(f32[1,4,32,512]{3,2,1,0:T(8,128)} %cot.1, f32[1,4,32,512]{3,2,1,0:T(8,128)} %pot.1, f32[4,512]{1,0:T(4,128)} %height.1), custom_call_target="tpu_custom_call" | custom-call | tf_op jit(solution)/shard_map/vcycle/pallas_call | solution.py:527
  38.0 0.7 %copy.7 = f32[1,4,32,512]{3,2,1,0:T(8,128)} copy(f32[1,4,32,512]{3,2,1,0:T(8,128)S(1)} %get-tuple-element.2) | data formatting | bytes 524288
  38.7 0.6 %copy.8 = f32[4,64]{1,0:T(4,128)} copy(f32[4,64]{1,0:T(4,128)S(1)} %get-tuple-element.3) | data formatting | bytes 2048

commit v4 on v3

--- a/solution.py
+++ b/solution.py
@@ -276,6 +276,11 @@
     field_copies = [
         send(fs.at[pl.ds(4, 4)], fs.at[pl.ds(4 - 4 * o, 4)], strip(o)) for o in (-1, 1)
     ]
+
+    pot_in.wait()
+    for x in range(0, 4):
+        spread_row(p_in, ps, x, x + 1)
+    potential_copies = [send(ps.at[1], ps.at[5], strip(-1)), send(ps.at[4], ps.at[0], strip(1))]
 
     def field_row(ref, slot):
         return [[ref[slot, p, pl.ds(q, 8, stride=4), :] for p in range(4)] for q in range(4)]
@@ -363,10 +368,6 @@
         send(packet.at[8], from_west3.at[0], strip(3)),
     ]
 
-    pot_in.wait()
-    for x in range(0, 4):
-        spread_row(p_in, ps, x, x + 1)
-
     for copy in d2_copies:
         copy.wait_recv()
     d2[0:8, :] = d2s[0]
@@ -384,16 +385,15 @@
     f2own[1] = (f2p[2] + from_west[1]) + (from_east[5] + from_west2[1]) + from_east2[0]
     f2own[2] = (f2p[3] + from_west[2]) + (from_east[6] + from_east2[1]) + from_east3[0]
     slots = (-9, -6, -3, 3, 6, 9)
-    row_copies = [send(f2own, f2r.at[slots.index(-o)], strip(o)) for o in (-9, 9, -6, 6, -3, 3)]
+    row_copies = [
+        send(f2own.at[pl.ds(0, 2)], f2r.at[5, pl.ds(0, 2)], strip(-9)),
+        send(f2own.at[pl.ds(1, 2)], f2r.at[0, pl.ds(1, 2)], strip(9)),
+    ]
+    row_copies += [send(f2own, f2r.at[slots.index(-o)], strip(o)) for o in (-6, 6, -3, 3)]
     for q in range(2):
         for p in range(2):
             f1[6, 2 * q + p] = f1p[1][q][p] + from_west[3 + 2 * q + p]
             f1[7, 2 * q + p] = f1p[2][q][p] + from_east[2 * q + p]
-    f1_copies = [send(f1.at[pl.ds(6, 2)], f1.at[pl.ds(6 - 2 * o, 2)], strip(o)) for o in (-1, 1, -2, 2)]
-    f1_copies += [send(f1.at[6], f1.at[12], strip(-3)), send(f1.at[7], f1.at[1], strip(3))]
-
-    potential_copies = [send(ps.at[1], ps.at[5], strip(-1)), send(ps.at[4], ps.at[0], strip(1))]
-
     terrain = terrain_weights(
         [ds[p, 8:24, :] for p in range(4)], [ds[p, 7:23, :] for p in range(4)], [ds[p, 9:25, :] for p in range(4)],
         *faces(16, 4, -4),
@@ -408,6 +408,8 @@
     for i in range(8, 12):
         guess_row(i)
     smooth_rows(v0, v1, 1, 11)
+    f1_copies = [send(f1.at[pl.ds(6, 2)], f1.at[pl.ds(6 - 2 * o, 2)], strip(o)) for o in (-1, 1, -2, 2)]
+    f1_copies += [send(f1.at[6], f1.at[12], strip(-3)), send(f1.at[7], f1.at[1], strip(3))]
 
     for copy in row_copies:
         copy.wait_recv()

time: 39.5 us -> 38.4 us (0.972)
  Pallas kernels: 37.4 us -> 36.3 us
    pallas_call x1, Pallas kernels: 37.4 us -> 36.3 us  [body(): pl.pallas_call(functools.partial(kernel, n_dir, n_gx), out_shape=(pltpu.V...]
where the time goes in v4:
time: 38.4 us; the launch traced here: 38.2 us
  Pallas kernels  36.3 us (95%)
  local copies, waits for them, and re-layouts  1.28 us (3%)
  between operations  0.64 us (2%)
    pallas_call x1, Pallas kernels, body(): pl.pallas_call(functools.partial(kernel, n_dir, n_gx), out_shape=(pltpu.V...  36.3 us
    unnamed x2, local copies, waits for them, and re-layouts  1.28 us

profile of v4, /device:TPU:1, one launch (start us, length us, event | category | flops | bytes accessed | tf_op | source)
XLA Modules:
  0.0 38.2 jit_solution(15724954686868441945)
XLA Ops:
  0.6 36.3 %vcycle.1 = (f32[1,4,32,512]{3,2,1,0:T(8,128)S(1)}, f32[4,64]{1,0:T(4,128)S(1)}) custom-call(f32[1,4,32,512]{3,2,1,0:T(8,128)} %cot.1, f32[1,4,32,512]{3,2,1,0:T(8,128)} %pot.1, f32[4,512]{1,0:T(4,128)} %height.1), custom_call_target="tpu_custom_call" | custom-call | tf_op jit(solution)/shard_map/vcycle/pallas_call | solution.py:529
  36.9 0.7 %copy.7 = f32[1,4,32,512]{3,2,1,0:T(8,128)} copy(f32[1,4,32,512]{3,2,1,0:T(8,128)S(1)} %get-tuple-element.2) | data formatting | bytes 524288
  37.6 0.6 %copy.8 = f32[4,64]{1,0:T(4,128)} copy(f32[4,64]{1,0:T(4,128)S(1)} %get-tuple-element.3) | data formatting | bytes 2048

commit v5 on v4

--- a/solution.py
+++ b/solution.py
@@ -213,19 +213,24 @@
     h_in, c_in, p_in, a_out, mixed,
     hs, fs, ps, ds, w0, de, d1, w1, df, d2s, d2, w2,
     v0, v1, v2, v3,
-    packet, from_west, from_east, from_west2, from_east2, from_west3, from_east3, f2own, f2r, f1, u0, u1, u2, u3,
+    packet, from_west, from_east, from_west2, from_east2, from_west3, from_east3, f2own, f2r, end_row, end_depth, f1, u0, u1, u2, u3,
     gn, er,
     local_sem, send_sem, recv_sem,
 ):
     me_dir, me = lax.axis_index("dir"), lax.axis_index("gx")
 
-    def strip(offset):
-        return {"gx": lax.rem(me + offset + 9 * n_gx, n_gx)}
+    def inside(offset):
+        return me + offset < n_gx if offset > 0 else me + offset >= 0
 
     barrier = pltpu.get_barrier_semaphore()
-    greeted = [o for s in range(1, GREET + 1) for o in (-s, s)]
-    for offset in greeted:
-        pl.semaphore_signal(barrier, inc=1, device_id=strip(offset), device_id_type=MESH)
+    greetings = n_dir - 1
+    for offset in [o for s in range(1, GREET + 1) for o in (-s, s)]:
+
+        @pl.when(inside(offset))
+        def _():
+            pl.semaphore_signal(barrier, inc=1, device_id={"gx": me + offset}, device_id_type=MESH)
+
+        greetings = greetings + inside(offset).astype(jnp.int32)
     for step in range(1, n_dir):
         pl.semaphore_signal(
             barrier, inc=1, device_id={"dir": lax.rem(me_dir + step, n_dir)}, device_id_type=MESH
@@ -238,17 +243,33 @@
     cot_in.start()
     pot_in.start()
 
-    sent = []
-
-    def send(source, target, device):
+    sent, by_offset = [], {}
+
+    def copy_to(source, target, device):
         index = len(sent)
         copy = pltpu.make_async_remote_copy(
             src_ref=source, dst_ref=target, send_sem=send_sem.at[index], recv_sem=recv_sem.at[index],
             device_id=device, device_id_type=MESH,
         )
-        copy.start()
         sent.append(copy)
         return copy
+
+    def send(source, target, offset):
+        copy = copy_to(source, target, {"gx": me + offset})
+        by_offset.setdefault(offset, []).append(copy)
+        pl.when(inside(offset))(copy.start)
+        return copy, target, offset
+
+    def arrive(copies, filler=0.0):
+        for copy, target, offset in copies:
+
+            @pl.when(inside(-offset))
+            def _():
+                copy.wait_recv()
+
+            @pl.when(jnp.logical_not(inside(-offset)))
+            def _():
+                target[...] = jnp.full(target.shape, filler, jnp.float32)
 
     bottom, top = iota((8, 128), 0) == 0, iota((8, 128), 0) == 7
 
@@ -262,8 +283,8 @@
     for p, cl in enumerate(spread_lanes([raw[:, 128 * c : 128 * c + 128] for c in range(4)])):
         hs[3, 4 * p : 4 * p + 4, :] = CEILING - cl
 
-    pl.semaphore_wait(barrier, len(greeted) + n_dir - 1)
-    depth_copies = [send(hs.at[3], hs.at[3 - o], strip(o)) for o in (-1, 1, -2, 2, -3, 3)]
+    pl.semaphore_wait(barrier, greetings)
+    depth_copies = [send(hs.at[3], hs.at[3 - o], o) for o in (-1, 1, -2, 2, -3, 3)]
 
     def spread_row(source, target, row, slot):
         block = source[row]
@@ -274,19 +295,18 @@
     for x in range(0, 4):
         spread_row(c_in, fs, x, x + 4)
     field_copies = [
-        send(fs.at[pl.ds(4, 4)], fs.at[pl.ds(4 - 4 * o, 4)], strip(o)) for o in (-1, 1)
+        send(fs.at[pl.ds(4, 4)], fs.at[pl.ds(4 - 4 * o, 4)], o) for o in (-1, 1)
     ]
 
     pot_in.wait()
     for x in range(0, 4):
         spread_row(p_in, ps, x, x + 1)
-    potential_copies = [send(ps.at[1], ps.at[5], strip(-1)), send(ps.at[4], ps.at[0], strip(1))]
+    potential_copies = [send(ps.at[1], ps.at[5], -1), send(ps.at[4], ps.at[0], 1)]
 
     def field_row(ref, slot):
         return [[ref[slot, p, pl.ds(q, 8, stride=4), :] for p in range(4)] for q in range(4)]
 
-    for copy in depth_copies:
-        copy.wait_recv()
+    arrive(depth_copies, 1.0)
     for o in range(7):
         for p in range(4):
             ds[p, 4 * o : 4 * o + 4, :] = hs[o, 4 * p : 4 * p + 4, :]
@@ -296,7 +316,13 @@
         d1[p1, 0:16, :] = 0.25 * (de[p1, pl.ds(0, 16, stride=2), :] + de[p1, pl.ds(1, 16, stride=2), :])
     df[...] = d1[0] + d1[1]
     d2s[1] = 0.25 * (df[pl.ds(0, 8, stride=2), :] + df[pl.ds(1, 8, stride=2), :])
-    d2_copies = [send(d2s.at[1], d2s.at[1 - s], strip(7 * s)) for s in (-1, 1)]
+    d2_copies = [send(d2s.at[1], d2s.at[1 - s], 7 * s) for s in (-1, 1)]
+    end_depths = []
+    for end, (home, sign) in enumerate(((0, 1), (n_gx - 1, -1))):
+        for away in (4, 5, 6):
+            copy = copy_to(d2s.at[1], end_depth.at[end], {"gx": me + sign * away})
+            pl.when(me == home)(copy.start)
+            end_depths.append((copy, end, home, home + sign * away, 7 - sign * away))
 
     def faces(rows, per_strip, first):
         size = n_gx * per_strip
@@ -360,36 +386,47 @@
     for k in range(5):
         packet[4 + k] = f2p[k]
     sum_copies = [
-        send(packet.at[pl.ds(0, 7)], from_east, strip(-1)),
-        send(packet.at[pl.ds(6, 7)], from_west, strip(1)),
-        send(packet.at[pl.ds(4, 2)], from_east2, strip(-2)),
-        send(packet.at[pl.ds(7, 2)], from_west2, strip(2)),
-        send(packet.at[4], from_east3.at[0], strip(-3)),
-        send(packet.at[8], from_west3.at[0], strip(3)),
-    ]
-
-    for copy in d2_copies:
-        copy.wait_recv()
+        send(packet.at[pl.ds(0, 7)], from_east, -1),
+        send(packet.at[pl.ds(6, 7)], from_west, 1),
+        send(packet.at[pl.ds(4, 2)], from_east2, -2),
+        send(packet.at[pl.ds(7, 2)], from_west2, 2),
+        send(packet.at[4], from_east3.at[0], -3),
+        send(packet.at[8], from_west3.at[0], 3),
+    ]
+
+    arrive(d2_copies, 1.0)
     d2[0:8, :] = d2s[0]
     d2[7:15, :] = d2s[1]
     d2[14:22, :] = d2s[2]
+    for copy, end, _, place, first in end_depths:
+
+        @pl.when(me == place)
+        def _():
+            copy.wait_recv()
+            d2[first : first + 7, :] = end_depth[end, 0:7, :]
+
     open_west, open_east = faces(24, 1, -9)
     for kind, value in enumerate(
         level_weights([d2[1:25, :]], [d2[0:24, :]], [d2[2:26, :]], open_west, open_east, 4.0)[0]
     ):
         w2[kind, 0] = value
 
-    for copy in sum_copies:
-        copy.wait_recv()
+    arrive(sum_copies)
     f2own[0] = (f2p[1] + from_west[0]) + (from_east[4] + from_west2[0]) + from_west3[0]
     f2own[1] = (f2p[2] + from_west[1]) + (from_east[5] + from_west2[1]) + from_east2[0]
     f2own[2] = (f2p[3] + from_west[2]) + (from_east[6] + from_east2[1]) + from_east3[0]
     slots = (-9, -6, -3, 3, 6, 9)
     row_copies = [
-        send(f2own.at[pl.ds(0, 2)], f2r.at[5, pl.ds(0, 2)], strip(-9)),
-        send(f2own.at[pl.ds(1, 2)], f2r.at[0, pl.ds(1, 2)], strip(9)),
-    ]
-    row_copies += [send(f2own, f2r.at[slots.index(-o)], strip(o)) for o in (-6, 6, -3, 3)]
+        send(f2own.at[pl.ds(0, 2)], f2r.at[5, pl.ds(0, 2)], -9),
+        send(f2own.at[pl.ds(1, 2)], f2r.at[0, pl.ds(1, 2)], 9),
+    ]
+    row_copies += [send(f2own, f2r.at[slots.index(-o)], o) for o in (-6, 6, -3, 3)]
+    end_copies = []
+    for end, (home, sign) in enumerate(((0, 1), (n_gx - 1, -1))):
+        for block in (3, 6, 9):
+            copy = copy_to(f2own.at[1], end_row.at[end], {"gx": me + sign * (block - 1)})
+            pl.when(me == home)(copy.start)
+            end_copies.append((copy, end, home, home + sign * (block - 1), slots.index(-sign * block)))
     for q in range(2):
         for p in range(2):
             f1[6, 2 * q + p] = f1p[1][q][p] + from_west[3 + 2 * q + p]
@@ -401,18 +438,23 @@
     for p, kinds in enumerate(terrain):
         for kind, value in enumerate(kinds):
             w0[GW + kind, p] = value
-    for copy in field_copies:
-        copy.wait_recv()
+    arrive(field_copies)
     for i in range(0, 4):
         guess_row(i)
     for i in range(8, 12):
         guess_row(i)
     smooth_rows(v0, v1, 1, 11)
-    f1_copies = [send(f1.at[pl.ds(6, 2)], f1.at[pl.ds(6 - 2 * o, 2)], strip(o)) for o in (-1, 1, -2, 2)]
-    f1_copies += [send(f1.at[6], f1.at[12], strip(-3)), send(f1.at[7], f1.at[1], strip(3))]
-
-    for copy in row_copies:
-        copy.wait_recv()
+    f1_copies = [send(f1.at[pl.ds(6, 2)], f1.at[pl.ds(6 - 2 * o, 2)], o) for o in (-1, 1, -2, 2)]
+    f1_copies += [send(f1.at[6], f1.at[12], -3), send(f1.at[7], f1.at[1], 3)]
+
+    arrive(row_copies)
+    for copy, end, _, place, slot in end_copies:
+
+        @pl.when(me == place)
+        def _():
+            copy.wait_recv()
+            f2r[slot, 2 - 2 * end] = end_row[end]
+
     start = []
     for o in range(-REACH, REACH + 1):
         block = (o + 10) // 3 * 3 - 9
@@ -425,8 +467,7 @@
             later[i] = swept(now[i], now[i - 1], now[i + 1], start[i], table(w2, i), bottom, top)
         now = later
 
-    for copy in f1_copies:
-        copy.wait_recv()
+    arrive(f1_copies)
     for i in range(0, 12):
         put_row(u0, i, first_guess(grid_of(f1[i + 1], 2), table(w1, i), bottom))
     for i in range(1, 11):
@@ -450,8 +491,7 @@
     smooth_rows(v1, v2, 2, 10)
     smooth_rows(v2, v3, 3, 9)
 
-    for copy in potential_copies:
-        copy.wait_recv()
+    arrive(potential_copies)
 
     def terrain_row(x):
         w = table(w0, x + 4)
@@ -481,7 +521,8 @@
     dir_copies = []
     for step in range(1, n_dir):
         target = lax.rem(me_dir + step, n_dir)
-        dir_copies.append(send(gn.at[target // (n_dir // 4)], er.at[step - 1], {"dir": target}))
+        dir_copies.append(copy_to(gn.at[target // (n_dir // 4)], er.at[step - 1], {"dir": target}))
+        dir_copies[-1].start()
 
     def natural_row(x):
         now_row = row_of(v3, x + 4)
@@ -509,8 +550,16 @@
     gradient[...] = mine[0:4, 0:width]
 
     out_copy.wait()
-    for copy in sent:
+    for copy in dir_copies:
         copy.wait_send()
+    for copy, _, home, _, _ in end_depths + end_copies:
+        pl.when(me == home)(copy.wait_send)
+    for offset, copies in by_offset.items():
+
+        @pl.when(inside(offset))
+        def _():
+            for copy in copies:
+                copy.wait_send()
 
 
 def body(cotangent, potential, height):
@@ -521,11 +570,11 @@
         (7, 16, 128), (12, 4, 32, 128), (6, 4, 32, 128), (4, 32, 128), (14, 4, 16, 128),
         (2, 32, 128), (2, 24, 128), (9, 2, 16, 128), (24, 128), (3, 8, 128), (32, 128), (9, 1, 24, 128),
         (12, 16, 8, 128), (12, 16, 8, 128), (12, 16, 8, 128), (12, 16, 8, 128),
-        (13, 8, 128), (7, 8, 128), (7, 8, 128), (2, 8, 128), (2, 8, 128), (1, 8, 128), (1, 8, 128), (3, 8, 128), (6, 3, 8, 128), (14, 4, 8, 128),
+        (13, 8, 128), (7, 8, 128), (7, 8, 128), (2, 8, 128), (2, 8, 128), (1, 8, 128), (1, 8, 128), (3, 8, 128), (6, 3, 8, 128), (2, 8, 128), (2, 8, 128), (14, 4, 8, 128),
         (12, 4, 8, 128), (12, 4, 8, 128), (12, 4, 8, 128), (12, 4, 8, 128),
         (4, 8, 128), (n_dir - 1, 8, 128),
     ]
-    copies = 6 + 2 + 2 + 2 + 6 + 6 + 6 + n_dir - 1
+    copies = 6 + 2 + 2 + 2 + 6 + 6 + 6 + 6 + 6 + n_dir - 1
     return pl.pallas_call(
         functools.partial(kernel, n_dir, n_gx),
         out_shape=(

time: 38.4 us -> 36.4 us (0.948)
  the two profiles are of different devices: /device:TPU:1 before, /device:TPU:6 now
where the time goes in v5:
time: 36.4 us; the launch traced here: 36 us
  Pallas kernels  34.1 us (94%)
  local copies, waits for them, and re-layouts  1.28 us (4%)
  between operations  0.64 us (2%)
    pallas_call x1, Pallas kernels, body(): pl.pallas_call(functools.partial(kernel, n_dir, n_gx), out_shape=(pltpu.V...  34.1 us
    unnamed x2, local copies, waits for them, and re-layouts  1.28 us

profile of v5, /device:TPU:6, one launch (start us, length us, event | category | flops | bytes accessed | tf_op | source)
XLA Modules:
  0.0 36.0 jit_solution(4372841155640896281)
XLA Ops:
  0.6 34.1 %vcycle.1 = (f32[1,4,32,512]{3,2,1,0:T(8,128)S(1)}, f32[4,64]{1,0:T(4,128)S(1)}) custom-call(f32[1,4,32,512]{3,2,1,0:T(8,128)} %cot.1, f32[1,4,32,512]{3,2,1,0:T(8,128)} %pot.1, f32[4,512]{1,0:T(4,128)} %height.1), custom_call_target="tpu_custom_call" | custom-call | tf_op jit(solution)/shard_map/vcycle/pallas_call | solution.py:578
  34.7 0.7 %copy.7 = f32[1,4,32,512]{3,2,1,0:T(8,128)} copy(f32[1,4,32,512]{3,2,1,0:T(8,128)S(1)} %get-tuple-element.2) | data formatting | bytes 524288
  35.4 0.6 %copy.8 = f32[4,64]{1,0:T(4,128)} copy(f32[4,64]{1,0:T(4,128)S(1)} %get-tuple-element.3) | data formatting | bytes 2048

commit v6 on v5

--- a/solution.py
+++ b/solution.py
@@ -213,8 +213,8 @@
     h_in, c_in, p_in, a_out, mixed,
     hs, fs, ps, ds, w0, de, d1, w1, df, d2s, d2, w2,
     v0, v1, v2, v3,
-    packet, from_west, from_east, from_west2, from_east2, from_west3, from_east3, f2own, f2r, end_row, end_depth, f1, u0, u1, u2, u3,
-    gn, er,
+    packet, from_west, from_east, from_west2, from_east2, from_west3, from_east3, f2own, f2r, end_row, end_depth, f1,
+    gn, er, es,
     local_sem, send_sem, recv_sem,
 ):
     me_dir, me = lax.axis_index("dir"), lax.axis_index("gx")
@@ -231,6 +231,16 @@
             pl.semaphore_signal(barrier, inc=1, device_id={"gx": me + offset}, device_id_type=MESH)
 
         greetings = greetings + inside(offset).astype(jnp.int32)
+
+    for offset in (-1, 1):
+
+        @pl.when(inside(offset))
+        def _():
+            for step in range(1, n_dir):
+                there = {"dir": lax.rem(me_dir + step, n_dir), "gx": me + offset}
+                pl.semaphore_signal(barrier, inc=1, device_id=there, device_id_type=MESH)
+
+        greetings = greetings + (n_dir - 1) * inside(offset).astype(jnp.int32)
     for step in range(1, n_dir):
         pl.semaphore_signal(
             barrier, inc=1, device_id={"dir": lax.rem(me_dir + step, n_dir)}, device_id_type=MESH
@@ -295,7 +305,8 @@
     for x in range(0, 4):
         spread_row(c_in, fs, x, x + 4)
     field_copies = [
-        send(fs.at[pl.ds(4, 4)], fs.at[pl.ds(4 - 4 * o, 4)], o) for o in (-1, 1)
+        send(fs.at[pl.ds(4, 3)], fs.at[pl.ds(8, 3)], -1),
+        send(fs.at[pl.ds(5, 3)], fs.at[pl.ds(1, 3)], 1),
     ]
 
     pot_in.wait()
@@ -439,13 +450,12 @@
         for kind, value in enumerate(kinds):
             w0[GW + kind, p] = value
     arrive(field_copies)
-    for i in range(0, 4):
+    for i in range(1, 4):
         guess_row(i)
-    for i in range(8, 12):
+    for i in range(8, 11):
         guess_row(i)
-    smooth_rows(v0, v1, 1, 11)
+    smooth_rows(v0, v1, 2, 10)
     f1_copies = [send(f1.at[pl.ds(6, 2)], f1.at[pl.ds(6 - 2 * o, 2)], o) for o in (-1, 1, -2, 2)]
-    f1_copies += [send(f1.at[6], f1.at[12], -3), send(f1.at[7], f1.at[1], 3)]
 
     arrive(row_copies)
     for copy, end, _, place, slot in end_copies:
@@ -468,64 +478,81 @@
         now = later
 
     arrive(f1_copies)
-    for i in range(0, 12):
-        put_row(u0, i, first_guess(grid_of(f1[i + 1], 2), table(w1, i), bottom))
-    for i in range(1, 11):
-        rows = [row_of(u0, i + d, 2) for d in (0, -1, 1)]
-        put_row(u1, i, swept(*rows, row_of(u0, i, 2), table(w1, i), bottom, top))
-    for i in range(1, 11):
+    begin = {i: first_guess(grid_of(f1[i + 1], 2), table(w1, i), bottom) for i in range(1, 11)}
+    fixed = {}
+    for i in range(2, 10):
         fix = now[(i - 5) // 2 + REACH][0][0]
-        put_row(u1, i, [[t + fix for t in line] for line in row_of(u1, i, 2)])
-    for source, target, low, high in ((u1, u2, 2, 10), (u2, u3, 3, 9)):
-        for i in range(low, high):
-            rows = [row_of(source, i + d, 2) for d in (0, -1, 1)]
-            put_row(target, i, swept(*rows, row_of(u0, i, 2), table(w1, i), bottom, top))
-
-    def corrected_row(i):
-        fix = row_of(u3, (i - 4 + 8) // 2 + 1, 2)
-        now_row = row_of(v1, i)
-        put_row(v1, i, [[now_row[q][p] + fix[q // 2][p // 2] for p in range(4)] for q in range(4)])
-
-    for i in range(1, 11):
-        corrected_row(i)
-    smooth_rows(v1, v2, 2, 10)
-    smooth_rows(v2, v3, 3, 9)
+        row = swept(begin[i], begin[i - 1], begin[i + 1], begin[i], table(w1, i), bottom, top)
+        fixed[i] = [[t + fix for t in line] for line in row]
+    for low, high in ((3, 9), (4, 8)):
+        fixed = {
+            i: swept(fixed[i], fixed[i - 1], fixed[i + 1], begin[i], table(w1, i), bottom, top) for i in range(low, high)
+        }
+
+    have = {i: row_of(v1, i) for i in range(2, 10)}
+    for i in range(2, 10):
+        fix = fixed[(i - 4 + 8) // 2 + 1]
+        put_row(v3, i, [[have[i][q][p] + fix[q // 2][p // 2] for p in range(4)] for q in range(4)])
+    smooth_rows(v3, v2, 3, 9)
+    smooth_rows(v2, v1, 4, 8)
 
     arrive(potential_copies)
 
     def terrain_row(x):
         w = table(w0, x + 4)
-        a, a_west, a_east = (row_of(v3, x + 4 + d) for d in (0, -1, 1))
+        a = row_of(v1, x + 4)
+        a_west, a_east = (row_of(v1, x + 4 + d) if 0 <= x + d <= 3 else None for d in (-1, 1))
         b, b_west, b_east = (field_row(ps, x + 1 + d) for d in (0, -1, 1))
         zeros = jnp.zeros((8, 128), jnp.float32)
         by_z, by_west, by_east, by_north = ([zeros] * 4 for _ in range(4))
         for q in range(4):
             for p in range(4):
                 by_z[p] += (above(a, q, p, top) - a[q][p]) * (above(b, q, p, top) - b[q][p])
-                by_west[p] += (a[q][p] - a_west[q][p]) * (b[q][p] - b_west[q][p])
-                by_east[p] += (a_east[q][p] - a[q][p]) * (b_east[q][p] - b[q][p])
+                rise = a[q][p] - a_west[q][p] if a_west else a[q][p]
+                by_west[p] += rise * (b[q][p] - b_west[q][p])
+                rise = a_east[q][p] - a[q][p] if a_east else -a[q][p]
+                by_east[p] += rise * (b_east[q][p] - b[q][p])
                 by_north[p] += (north_of(a, q, p) - a[q][p]) * (north_of(b, q, p) - b[q][p])
         out = []
         for p in range(4):
             by_south = by_north[p - 1] if p else pltpu.roll(by_north[3], 1, 1)
             total = w(GW, p) * by_west[p] + w(GE, p) * by_east[p] + w(GN, p) * by_north[p]
             total = total + w(GS, p) * by_south + w(GZ, p) * by_z[p]
-            out.append(jnp.sum(total, axis=0, keepdims=True))
-        return out
-
-    sums = [terrain_row(x) for x in range(4)]
-    blank = jnp.zeros((4, 128), jnp.float32)
-    packed = [jnp.concatenate([sums[x][p] for x in range(4)] + [blank], axis=0) for p in range(4)]
+            out.append(total)
+        if x == 0:
+            parts[0] = [table(w0, 3)(GE, p) * by_west[p] for p in range(4)]
+        if x == 3:
+            parts[5] = [table(w0, 8)(GW, p) * by_east[p] for p in range(4)]
+        parts[x + 1] = out
+
+    parts = {}
+    for x in range(4):
+        terrain_row(x)
+    blank = jnp.zeros((2, 128), jnp.float32)
+    packed = [
+        jnp.concatenate([jnp.sum(parts[k][p], axis=0, keepdims=True) for k in range(6)] + [blank], axis=0) for p in range(4)
+    ]
     for c, tile in enumerate(join_lanes(packed)):
         gn[c] = tile
-    dir_copies = []
-    for step in range(1, n_dir):
+    dir_copies, side_copies = [], {-1: [], 1: []}
+    for step in range(n_dir):
         target = lax.rem(me_dir + step, n_dir)
-        dir_copies.append(copy_to(gn.at[target // (n_dir // 4)], er.at[step - 1], {"dir": target}))
-        dir_copies[-1].start()
+        source = gn.at[target // (n_dir // 4)]
+        if step:
+            dir_copies.append(copy_to(source, er.at[step - 1], {"dir": target}))
+            dir_copies[-1].start()
+        for offset, slot in ((-1, 1), (1, 0)):
+            there = {"dir": target, "gx": me + offset}
+            side_copies[offset].append(copy_to(source, es.at[slot, step], there))
+    for offset in (-1, 1):
+
+        @pl.when(inside(offset))
+        def _():
+            for copy in side_copies[offset]:
+                copy.start()
 
     def natural_row(x):
-        now_row = row_of(v3, x + 4)
+        now_row = row_of(v1, x + 4)
         for p in range(4):
             for q in range(4):
                 mixed[x, p, pl.ds(q, 8, stride=4), :] = now_row[q][p]
@@ -542,16 +569,38 @@
     total = gn[me_dir // (n_dir // 4)]
     for step in range(1, n_dir):
         total = total + er[step - 1]
+    for offset, slot, row, place in ((1, 0, 5, 1), (-1, 1, 0, 4)):
+
+        @pl.when(inside(-offset))
+        def _():
+            for copy in side_copies[offset]:
+                copy.wait_recv()
+
+        @pl.when(jnp.logical_not(inside(-offset)))
+        def _():
+            es[slot] = jnp.zeros(es.shape[1:], jnp.float32)
+
+        side = es[slot, 0]
+        for step in range(1, n_dir):
+            side = side + es[slot, step]
+        total = total + jnp.where(iota((8, 128), 0) == place, pltpu.roll(side, (place - row) % 8, 0), 0.0)
     part = lax.rem(me_dir, n_dir // 4)
     mine = total
     width = gradient.shape[1]
     for k in range(1, 128 // width):
         mine = jnp.where(iota((8, 128), 0) * 0 + part == k, pltpu.roll(total, 128 - k * width, 1), mine)
-    gradient[...] = mine[0:4, 0:width]
+    gradient[...] = mine[1:5, 0:width]
 
     out_copy.wait()
     for copy in dir_copies:
         copy.wait_send()
+    for offset in (-1, 1):
+
+        @pl.when(inside(offset))
+        def _():
+            for copy in side_copies[offset]:
+                copy.wait_send()
+
     for copy, _, home, _, _ in end_depths + end_copies:
         pl.when(me == home)(copy.wait_send)
     for offset, copies in by_offset.items():
@@ -571,10 +620,9 @@
         (2, 32, 128), (2, 24, 128), (9, 2, 16, 128), (24, 128), (3, 8, 128), (32, 128), (9, 1, 24, 128),
         (12, 16, 8, 128), (12, 16, 8, 128), (12, 16, 8, 128), (12, 16, 8, 128),
         (13, 8, 128), (7, 8, 128), (7, 8, 128), (2, 8, 128), (2, 8, 128), (1, 8, 128), (1, 8, 128), (3, 8, 128), (6, 3, 8, 128), (2, 8, 128), (2, 8, 128), (14, 4, 8, 128),
-        (12, 4, 8, 128), (12, 4, 8, 128), (12, 4, 8, 128), (12, 4, 8, 128),
-        (4, 8, 128), (n_dir - 1, 8, 128),
-    ]
-    copies = 6 + 2 + 2 + 2 + 6 + 6 + 6 + 6 + 6 + n_dir - 1
+        (4, 8, 128), (n_dir - 1, 8, 128), (2, n_dir, 8, 128),
+    ]
+    copies = 6 + 2 + 2 + 2 + 6 + 6 + 6 + 6 + 4 + n_dir - 1 + 2 * n_dir
     return pl.pallas_call(
         functools.partial(kernel, n_dir, n_gx),
         out_shape=(

time: 36.4 us -> 37.6 us (1.033)
  Pallas kernels: 34.1 us -> 35.3 us
    pallas_call x1, Pallas kernels: 34.1 us -> 35.3 us  [body(): pl.pallas_call(functools.partial(kernel, n_dir, n_gx), out_shape=(pltpu.V...]
where the time goes in v6:
time: 37.6 us; the launch traced here: 37.2 us
  Pallas kernels  35.3 us (94%)
  local copies, waits for them, and re-layouts  1.28 us (3%)
  between operations  0.64 us (2%)
    pallas_call x1, Pallas kernels, body(): pl.pallas_call(functools.partial(kernel, n_dir, n_gx), out_shape=(pltpu.V...  35.3 us
    unnamed x2, local copies, waits for them, and re-layouts  1.28 us

profile of v6, /device:TPU:6, one launch (start us, length us, event | category | flops | bytes accessed | tf_op | source)
XLA Modules:
  0.0 37.2 jit_solution(11773322971727272008)
XLA Ops:
  0.6 35.3 %vcycle.1 = (f32[1,4,32,512]{3,2,1,0:T(8,128)S(1)}, f32[4,64]{1,0:T(4,128)S(1)}) custom-call(f32[1,4,32,512]{3,2,1,0:T(8,128)} %cot.1, f32[1,4,32,512]{3,2,1,0:T(8,128)} %pot.1, f32[4,512]{1,0:T(4,128)} %height.1), custom_call_target="tpu_custom_call" | custom-call | tf_op jit(solution)/shard_map/vcycle/pallas_call | solution.py:626
  35.9 0.7 %copy.7 = f32[1,4,32,512]{3,2,1,0:T(8,128)} copy(f32[1,4,32,512]{3,2,1,0:T(8,128)S(1)} %get-tuple-element.2) | data formatting | bytes 524288
  36.6 0.6 %copy.8 = f32[4,64]{1,0:T(4,128)} copy(f32[4,64]{1,0:T(4,128)S(1)} %get-tuple-element.3) | data formatting | bytes 2048

commit v7 on v5

--- a/solution.py
+++ b/solution.py
@@ -213,7 +213,7 @@
     h_in, c_in, p_in, a_out, mixed,
     hs, fs, ps, ds, w0, de, d1, w1, df, d2s, d2, w2,
     v0, v1, v2, v3,
-    packet, from_west, from_east, from_west2, from_east2, from_west3, from_east3, f2own, f2r, end_row, end_depth, f1, u0, u1, u2, u3,
+    packet, from_west, from_east, from_west2, from_east2, from_west3, from_east3, f2own, f2r, end_row, end_depth, f1,
     gn, er,
     local_sem, send_sem, recv_sem,
 ):
@@ -260,16 +260,32 @@
         pl.when(inside(offset))(copy.start)
         return copy, target, offset
 
-    def arrive(copies, filler=0.0):
-        for copy, target, offset in copies:
-
-            @pl.when(inside(-offset))
-            def _():
-                copy.wait_recv()
-
-            @pl.when(jnp.logical_not(inside(-offset)))
-            def _():
-                target[...] = jnp.full(target.shape, filler, jnp.float32)
+    def arrive(copies):
+        for copy, _, offset in copies:
+            pl.when(inside(-offset))(copy.wait_recv)
+
+    slots = (-9, -6, -3, 3, 6, 9)
+    for offset, ones, zeros in (
+        (-1, (hs.at[2],), (fs.at[pl.ds(0, 4)], ps.at[0], from_west, f1.at[pl.ds(4, 2)])),
+        (1, (hs.at[4],), (fs.at[pl.ds(8, 4)], ps.at[5], from_east, f1.at[pl.ds(8, 2)])),
+        (-2, (hs.at[1],), (from_west2, f1.at[pl.ds(2, 2)])),
+        (2, (hs.at[5],), (from_east2, f1.at[pl.ds(10, 2)])),
+        (-3, (hs.at[0],), (from_west3, f1.at[1], f2r.at[2])),
+        (3, (hs.at[6],), (from_east3, f1.at[12], f2r.at[3])),
+        (-6, (), (f2r.at[1],)),
+        (6, (), (f2r.at[4],)),
+        (-7, (d2s.at[0],), ()),
+        (7, (d2s.at[2],), ()),
+        (-9, (), (f2r.at[0, pl.ds(1, 2)],)),
+        (9, (), (f2r.at[5, pl.ds(0, 2)],)),
+    ):
+
+        @pl.when(jnp.logical_not(inside(offset)))
+        def _():
+            for ref in ones:
+                ref[...] = jnp.ones(ref.shape, jnp.float32)
+            for ref in zeros:
+                ref[...] = jnp.zeros(ref.shape, jnp.float32)
 
     bottom, top = iota((8, 128), 0) == 0, iota((8, 128), 0) == 7
 
@@ -284,7 +300,7 @@
         hs[3, 4 * p : 4 * p + 4, :] = CEILING - cl
 
     pl.semaphore_wait(barrier, greetings)
-    depth_copies = [send(hs.at[3], hs.at[3 - o], o) for o in (-1, 1, -2, 2, -3, 3)]
+    depth_copies = [send(hs.at[3], hs.at[3 - o], o) for o in (-3, 3, -2, 2, -1, 1)]
 
     def spread_row(source, target, row, slot):
         block = source[row]
@@ -306,7 +322,7 @@
     def field_row(ref, slot):
         return [[ref[slot, p, pl.ds(q, 8, stride=4), :] for p in range(4)] for q in range(4)]
 
-    arrive(depth_copies, 1.0)
+    arrive(depth_copies)
     for o in range(7):
         for p in range(4):
             ds[p, 4 * o : 4 * o + 4, :] = hs[o, 4 * p : 4 * p + 4, :]
@@ -316,14 +332,6 @@
         d1[p1, 0:16, :] = 0.25 * (de[p1, pl.ds(0, 16, stride=2), :] + de[p1, pl.ds(1, 16, stride=2), :])
     df[...] = d1[0] + d1[1]
     d2s[1] = 0.25 * (df[pl.ds(0, 8, stride=2), :] + df[pl.ds(1, 8, stride=2), :])
-    d2_copies = [send(d2s.at[1], d2s.at[1 - s], 7 * s) for s in (-1, 1)]
-    end_depths = []
-    for end, (home, sign) in enumerate(((0, 1), (n_gx - 1, -1))):
-        for away in (4, 5, 6):
-            copy = copy_to(d2s.at[1], end_depth.at[end], {"gx": me + sign * away})
-            pl.when(me == home)(copy.start)
-            end_depths.append((copy, end, home, home + sign * away, 7 - sign * away))
-
     def faces(rows, per_strip, first):
         size = n_gx * per_strip
         place = (me * per_strip + first + REACH * size + iota((rows, 128), 0)) & (size - 1)
@@ -394,28 +402,18 @@
         send(packet.at[8], from_west3.at[0], 3),
     ]
 
-    arrive(d2_copies, 1.0)
-    d2[0:8, :] = d2s[0]
-    d2[7:15, :] = d2s[1]
-    d2[14:22, :] = d2s[2]
-    for copy, end, _, place, first in end_depths:
-
-        @pl.when(me == place)
-        def _():
-            copy.wait_recv()
-            d2[first : first + 7, :] = end_depth[end, 0:7, :]
-
-    open_west, open_east = faces(24, 1, -9)
-    for kind, value in enumerate(
-        level_weights([d2[1:25, :]], [d2[0:24, :]], [d2[2:26, :]], open_west, open_east, 4.0)[0]
-    ):
-        w2[kind, 0] = value
+    d2_copies = [send(d2s.at[1], d2s.at[1 - s], 7 * s) for s in (-1, 1)]
+    end_depths = []
+    for end, (home, sign) in enumerate(((0, 1), (n_gx - 1, -1))):
+        for away in (4, 5, 6):
+            copy = copy_to(d2s.at[1], end_depth.at[end], {"gx": me + sign * away})
+            pl.when(me == home)(copy.start)
+            end_depths.append((copy, end, home, home + sign * away, 7 - sign * away))
 
     arrive(sum_copies)
     f2own[0] = (f2p[1] + from_west[0]) + (from_east[4] + from_west2[0]) + from_west3[0]
     f2own[1] = (f2p[2] + from_west[1]) + (from_east[5] + from_west2[1]) + from_east2[0]
     f2own[2] = (f2p[3] + from_west[2]) + (from_east[6] + from_east2[1]) + from_east3[0]
-    slots = (-9, -6, -3, 3, 6, 9)
     row_copies = [
         send(f2own.at[pl.ds(0, 2)], f2r.at[5, pl.ds(0, 2)], -9),
         send(f2own.at[pl.ds(1, 2)], f2r.at[0, pl.ds(1, 2)], 9),
@@ -431,6 +429,23 @@
         for p in range(2):
             f1[6, 2 * q + p] = f1p[1][q][p] + from_west[3 + 2 * q + p]
             f1[7, 2 * q + p] = f1p[2][q][p] + from_east[2 * q + p]
+    arrive(d2_copies)
+    d2[0:8, :] = d2s[0]
+    d2[7:15, :] = d2s[1]
+    d2[14:22, :] = d2s[2]
+    for copy, end, _, place, first in end_depths:
+
+        @pl.when(me == place)
+        def _():
+            copy.wait_recv()
+            d2[first : first + 7, :] = end_depth[end, 0:7, :]
+
+    open_west, open_east = faces(24, 1, -9)
+    for kind, value in enumerate(
+        level_weights([d2[1:25, :]], [d2[0:24, :]], [d2[2:26, :]], open_west, open_east, 4.0)[0]
+    ):
+        w2[kind, 0] = value
+
     terrain = terrain_weights(
         [ds[p, 8:24, :] for p in range(4)], [ds[p, 7:23, :] for p in range(4)], [ds[p, 9:25, :] for p in range(4)],
         *faces(16, 4, -4),
@@ -468,34 +483,29 @@
         now = later
 
     arrive(f1_copies)
-    for i in range(0, 12):
-        put_row(u0, i, first_guess(grid_of(f1[i + 1], 2), table(w1, i), bottom))
-    for i in range(1, 11):
-        rows = [row_of(u0, i + d, 2) for d in (0, -1, 1)]
-        put_row(u1, i, swept(*rows, row_of(u0, i, 2), table(w1, i), bottom, top))
+    begin = {i: first_guess(grid_of(f1[i + 1], 2), table(w1, i), bottom) for i in range(0, 12)}
+    fixed = {}
     for i in range(1, 11):
         fix = now[(i - 5) // 2 + REACH][0][0]
-        put_row(u1, i, [[t + fix for t in line] for line in row_of(u1, i, 2)])
-    for source, target, low, high in ((u1, u2, 2, 10), (u2, u3, 3, 9)):
-        for i in range(low, high):
-            rows = [row_of(source, i + d, 2) for d in (0, -1, 1)]
-            put_row(target, i, swept(*rows, row_of(u0, i, 2), table(w1, i), bottom, top))
-
-    def corrected_row(i):
-        fix = row_of(u3, (i - 4 + 8) // 2 + 1, 2)
-        now_row = row_of(v1, i)
-        put_row(v1, i, [[now_row[q][p] + fix[q // 2][p // 2] for p in range(4)] for q in range(4)])
-
+        row = swept(begin[i], begin[i - 1], begin[i + 1], begin[i], table(w1, i), bottom, top)
+        fixed[i] = [[t + fix for t in line] for line in row]
+    for low, high in ((2, 10), (3, 9)):
+        fixed = {
+            i: swept(fixed[i], fixed[i - 1], fixed[i + 1], begin[i], table(w1, i), bottom, top) for i in range(low, high)
+        }
+
+    have = {i: row_of(v1, i) for i in range(1, 11)}
     for i in range(1, 11):
-        corrected_row(i)
-    smooth_rows(v1, v2, 2, 10)
-    smooth_rows(v2, v3, 3, 9)
+        fix = fixed[(i - 4 + 8) // 2 + 1]
+        put_row(v3, i, [[have[i][q][p] + fix[q // 2][p // 2] for p in range(4)] for q in range(4)])
+    smooth_rows(v3, v2, 2, 10)
+    smooth_rows(v2, v1, 3, 9)
 
     arrive(potential_copies)
 
     def terrain_row(x):
         w = table(w0, x + 4)
-        a, a_west, a_east = (row_of(v3, x + 4 + d) for d in (0, -1, 1))
+        a, a_west, a_east = (row_of(v1, x + 4 + d) for d in (0, -1, 1))
         b, b_west, b_east = (field_row(ps, x + 1 + d) for d in (0, -1, 1))
         zeros = jnp.zeros((8, 128), jnp.float32)
         by_z, by_west, by_east, by_north = ([zeros] * 4 for _ in range(4))
@@ -519,13 +529,13 @@
     for c, tile in enumerate(join_lanes(packed)):
         gn[c] = tile
     dir_copies = []
-    for step in range(1, n_dir):
+    for step in sorted(range(1, n_dir), key=lambda k: abs(2 * k - n_dir)):
         target = lax.rem(me_dir + step, n_dir)
         dir_copies.append(copy_to(gn.at[target // (n_dir // 4)], er.at[step - 1], {"dir": target}))
         dir_copies[-1].start()
 
     def natural_row(x):
-        now_row = row_of(v3, x + 4)
+        now_row = row_of(v1, x + 4)
         for p in range(4):
             for q in range(4):
                 mixed[x, p, pl.ds(q, 8, stride=4), :] = now_row[q][p]
@@ -536,6 +546,15 @@
         natural_row(i)
     out_copy = pltpu.make_async_copy(a_out, adjoint.at[0], local_sem.at[3])
     out_copy.start()
+
+    for copy, _, home, _, _ in end_depths + end_copies:
+        pl.when(me == home)(copy.wait_send)
+    for offset, copies in by_offset.items():
+
+        @pl.when(inside(offset))
+        def _():
+            for copy in copies:
+                copy.wait_send()
 
     for copy in dir_copies:
         copy.wait_recv()
@@ -552,14 +571,6 @@
     out_copy.wait()
     for copy in dir_copies:
         copy.wait_send()
-    for copy, _, home, _, _ in end_depths + end_copies:
-        pl.when(me == home)(copy.wait_send)
-    for offset, copies in by_offset.items():
-
-        @pl.when(inside(offset))
-        def _():
-            for copy in copies:
-                copy.wait_send()
 
 
 def body(cotangent, potential, height):
@@ -571,7 +582,6 @@
         (2, 32, 128), (2, 24, 128), (9, 2, 16, 128), (24, 128), (3, 8, 128), (32, 128), (9, 1, 24, 128),
         (12, 16, 8, 128), (12, 16, 8, 128), (12, 16, 8, 128), (12, 16, 8, 128),
         (13, 8, 128), (7, 8, 128), (7, 8, 128), (2, 8, 128), (2, 8, 128), (1, 8, 128), (1, 8, 128), (3, 8, 128), (6, 3, 8, 128), (2, 8, 128), (2, 8, 128), (14, 4, 8, 128),
-        (12, 4, 8, 128), (12, 4, 8, 128), (12, 4, 8, 128), (12, 4, 8, 128),
         (4, 8, 128), (n_dir - 1, 8, 128),
     ]
     copies = 6 + 2 + 2 + 2 + 6 + 6 + 6 + 6 + 6 + n_dir - 1

time: 36.4 us -> 35.9 us (0.986)
  Pallas kernels: 34.1 us -> 33.5 us
    pallas_call x1, Pallas kernels: 34.1 us -> 33.5 us  [body(): pl.pallas_call(functools.partial(kernel, n_dir, n_gx), out_shape=(pltpu.V...]
where the time goes in v7:
time: 35.9 us; the launch traced here: 35.5 us
  Pallas kernels  33.5 us (93%)
  local copies, waits for them, and re-layouts  1.28 us (4%)
  between operations  0.64 us (2%)
    pallas_call x1, Pallas kernels, body(): pl.pallas_call(functools.partial(kernel, n_dir, n_gx), out_shape=(pltpu.V...  33.5 us
    unnamed x2, local copies, waits for them, and re-layouts  1.28 us

profile of v7, /device:TPU:6, one launch (start us, length us, event | category | flops | bytes accessed | tf_op | source)
XLA Modules:
  0.0 35.5 jit_solution(16477699851439102114)
XLA Ops:
  0.6 33.5 %vcycle.1 = (f32[1,4,32,512]{3,2,1,0:T(8,128)S(1)}, f32[4,64]{1,0:T(4,128)S(1)}) custom-call(f32[1,4,32,512]{3,2,1,0:T(8,128)} %cot.1, f32[1,4,32,512]{3,2,1,0:T(8,128)} %pot.1, f32[4,512]{1,0:T(4,128)} %height.1), custom_call_target="tpu_custom_call" | custom-call | tf_op jit(solution)/shard_map/vcycle/pallas_call | solution.py:588
  34.2 0.7 %copy.7 = f32[1,4,32,512]{3,2,1,0:T(8,128)} copy(f32[1,4,32,512]{3,2,1,0:T(8,128)S(1)} %get-tuple-element.2) | data formatting | bytes 524288
  34.9 0.6 %copy.8 = f32[4,64]{1,0:T(4,128)} copy(f32[4,64]{1,0:T(4,128)S(1)} %get-tuple-element.3) | data formatting | bytes 2048

commit v8 on v7

--- a/solution.py
+++ b/solution.py
@@ -254,11 +254,20 @@
         sent.append(copy)
         return copy
 
-    def send(source, target, offset):
+    def send(source, target, offset, start=True):
         copy = copy_to(source, target, {"gx": me + offset})
         by_offset.setdefault(offset, []).append(copy)
-        pl.when(inside(offset))(copy.start)
+        if start:
+            pl.when(inside(offset))(copy.start)
         return copy, target, offset
+
+    def send_sides(to_west, to_east):
+        copies = [send(*to_west, -1, start=False), send(*to_east, 1, start=False)]
+        odd = lax.rem(me, 2) == 1
+        pl.when(odd & inside(1))(copies[1][0].start)
+        pl.when(inside(-1))(copies[0][0].start)
+        pl.when(jnp.logical_not(odd) & inside(1))(copies[1][0].start)
+        return copies
 
     def arrive(copies):
         for copy, _, offset in copies:
@@ -310,14 +319,12 @@
     cot_in.wait()
     for x in range(0, 4):
         spread_row(c_in, fs, x, x + 4)
-    field_copies = [
-        send(fs.at[pl.ds(4, 4)], fs.at[pl.ds(4 - 4 * o, 4)], o) for o in (-1, 1)
-    ]
+    field_copies = send_sides((fs.at[pl.ds(4, 4)], fs.at[pl.ds(8, 4)]), (fs.at[pl.ds(4, 4)], fs.at[pl.ds(0, 4)]))
 
     pot_in.wait()
     for x in range(0, 4):
         spread_row(p_in, ps, x, x + 1)
-    potential_copies = [send(ps.at[1], ps.at[5], -1), send(ps.at[4], ps.at[0], 1)]
+    potential_copies = send_sides((ps.at[1], ps.at[5]), (ps.at[4], ps.at[0]))
 
     def field_row(ref, slot):
         return [[ref[slot, p, pl.ds(q, 8, stride=4), :] for p in range(4)] for q in range(4)]
@@ -453,14 +460,14 @@
     for p, kinds in enumerate(terrain):
         for kind, value in enumerate(kinds):
             w0[GW + kind, p] = value
+    f1_copies = [send(f1.at[pl.ds(6, 2)], f1.at[pl.ds(6 - 2 * o, 2)], o) for o in (-1, 1, -2, 2)]
+    f1_copies += [send(f1.at[6], f1.at[12], -3), send(f1.at[7], f1.at[1], 3)]
     arrive(field_copies)
     for i in range(0, 4):
         guess_row(i)
     for i in range(8, 12):
         guess_row(i)
     smooth_rows(v0, v1, 1, 11)
-    f1_copies = [send(f1.at[pl.ds(6, 2)], f1.at[pl.ds(6 - 2 * o, 2)], o) for o in (-1, 1, -2, 2)]
-    f1_copies += [send(f1.at[6], f1.at[12], -3), send(f1.at[7], f1.at[1], 3)]
 
     arrive(row_copies)
     for copy, end, _, place, slot in end_copies:

time: 35.9 us -> 35.6 us (level)
  no operation moved by 1% of the time
where the time goes in v8:
time: 35.6 us; the launch traced here: 35.1 us
  Pallas kernels  33.2 us (93%)
  local copies, waits for them, and re-layouts  1.28 us (4%)
  between operations  0.64 us (2%)
    pallas_call x1, Pallas kernels, body(): pl.pallas_call(functools.partial(kernel, n_dir, n_gx), out_shape=(pltpu.V...  33.2 us
    unnamed x2, local copies, waits for them, and re-layouts  1.28 us

profile of v8, /device:TPU:6, one launch (start us, length us, event | category | flops | bytes accessed | tf_op | source)
XLA Modules:
  0.0 35.1 jit_solution(14067440089538525186)
XLA Ops:
  0.6 33.2 %vcycle.1 = (f32[1,4,32,512]{3,2,1,0:T(8,128)S(1)}, f32[4,64]{1,0:T(4,128)S(1)}) custom-call(f32[1,4,32,512]{3,2,1,0:T(8,128)} %cot.1, f32[1,4,32,512]{3,2,1,0:T(8,128)} %pot.1, f32[4,512]{1,0:T(4,128)} %height.1), custom_call_target="tpu_custom_call" | custom-call | tf_op jit(solution)/shard_map/vcycle/pallas_call | solution.py:595
  33.9 0.7 %copy.7 = f32[1,4,32,512]{3,2,1,0:T(8,128)} copy(f32[1,4,32,512]{3,2,1,0:T(8,128)S(1)} %get-tuple-element.2) | data formatting | bytes 524288
  34.6 0.6 %copy.8 = f32[4,64]{1,0:T(4,128)} copy(f32[4,64]{1,0:T(4,128)S(1)} %get-tuple-element.3) | data formatting | bytes 2048

commit v9 on v8

--- a/solution.py
+++ b/solution.py
@@ -219,29 +219,29 @@
 ):
     me_dir, me = lax.axis_index("dir"), lax.axis_index("gx")
 
-    def inside(offset):
-        return me + offset < n_gx if offset > 0 else me + offset >= 0
-
-    barrier = pltpu.get_barrier_semaphore()
-    greetings = n_dir - 1
-    for offset in [o for s in range(1, GREET + 1) for o in (-s, s)]:
-
-        @pl.when(inside(offset))
-        def _():
-            pl.semaphore_signal(barrier, inc=1, device_id={"gx": me + offset}, device_id_type=MESH)
-
-        greetings = greetings + inside(offset).astype(jnp.int32)
-    for step in range(1, n_dir):
-        pl.semaphore_signal(
-            barrier, inc=1, device_id={"dir": lax.rem(me_dir + step, n_dir)}, device_id_type=MESH
-        )
-
     height_in = pltpu.make_async_copy(height, h_in, local_sem.at[0])
     cot_in = pltpu.make_async_copy(cot.at[0], c_in, local_sem.at[1])
     pot_in = pltpu.make_async_copy(pot.at[0], p_in, local_sem.at[2])
     height_in.start()
     cot_in.start()
     pot_in.start()
+
+    def inside(offset):
+        return me + offset < n_gx if offset > 0 else me + offset >= 0
+
+    barrier = pltpu.get_barrier_semaphore()
+    greetings = n_dir - 1
+    for offset in [o for s in range(1, GREET + 1) for o in (-s, s)]:
+
+        @pl.when(inside(offset))
+        def _():
+            pl.semaphore_signal(barrier, inc=1, device_id={"gx": me + offset}, device_id_type=MESH)
+
+        greetings = greetings + inside(offset).astype(jnp.int32)
+    for step in range(1, n_dir):
+        pl.semaphore_signal(
+            barrier, inc=1, device_id={"dir": lax.rem(me_dir + step, n_dir)}, device_id_type=MESH
+        )
 
     sent, by_offset = [], {}
 
@@ -320,11 +320,6 @@
     for x in range(0, 4):
         spread_row(c_in, fs, x, x + 4)
     field_copies = send_sides((fs.at[pl.ds(4, 4)], fs.at[pl.ds(8, 4)]), (fs.at[pl.ds(4, 4)], fs.at[pl.ds(0, 4)]))
-
-    pot_in.wait()
-    for x in range(0, 4):
-        spread_row(p_in, ps, x, x + 1)
-    potential_copies = send_sides((ps.at[1], ps.at[5]), (ps.at[4], ps.at[0]))
 
     def field_row(ref, slot):
         return [[ref[slot, p, pl.ds(q, 8, stride=4), :] for p in range(4)] for q in range(4)]
@@ -416,6 +411,10 @@
             copy = copy_to(d2s.at[1], end_depth.at[end], {"gx": me + sign * away})
             pl.when(me == home)(copy.start)
             end_depths.append((copy, end, home, home + sign * away, 7 - sign * away))
+
+    pot_in.wait()
+    for x in range(0, 4):
+        spread_row(p_in, ps, x, x + 1)
 
     arrive(sum_copies)
     f2own[0] = (f2p[1] + from_west[0]) + (from_east[4] + from_west2[0]) + from_west3[0]
@@ -468,6 +467,7 @@
     for i in range(8, 12):
         guess_row(i)
     smooth_rows(v0, v1, 1, 11)
+    potential_copies = send_sides((ps.at[1], ps.at[5]), (ps.at[4], ps.at[0]))
 
     arrive(row_copies)
     for copy, end, _, place, slot in end_copies:

time: 35.6 us -> 35.6 us (level)
  no operation moved by 1% of the time
where the time goes in v9:
time: 35.6 us; the launch traced here: 35.4 us
  Pallas kernels  33.5 us (94%)
  local copies, waits for them, and re-layouts  1.28 us (4%)
  between operations  0.64 us (2%)
    pallas_call x1, Pallas kernels, body(): pl.pallas_call(functools.partial(kernel, n_dir, n_gx), out_shape=(pltpu.V...  33.5 us
    unnamed x2, local copies, waits for them, and re-layouts  1.28 us

profile of v9, /device:TPU:6, one launch (start us, length us, event | category | flops | bytes accessed | tf_op | source)
XLA Modules:
  0.0 35.4 jit_solution(1971057968088676781)
XLA Ops:
  0.6 33.5 %vcycle.1 = (f32[1,4,32,512]{3,2,1,0:T(8,128)S(1)}, f32[4,64]{1,0:T(4,128)S(1)}) custom-call(f32[1,4,32,512]{3,2,1,0:T(8,128)} %cot.1, f32[1,4,32,512]{3,2,1,0:T(8,128)} %pot.1, f32[4,512]{1,0:T(4,128)} %height.1), custom_call_target="tpu_custom_call" | custom-call | tf_op jit(solution)/shard_map/vcycle/pallas_call | solution.py:595
  34.1 0.7 %copy.7 = f32[1,4,32,512]{3,2,1,0:T(8,128)} copy(f32[1,4,32,512]{3,2,1,0:T(8,128)S(1)} %get-tuple-element.2) | data formatting | bytes 524288
  34.8 0.6 %copy.8 = f32[4,64]{1,0:T(4,128)} copy(f32[4,64]{1,0:T(4,128)S(1)} %get-tuple-element.3) | data formatting | bytes 2048
